TPU v7x, 32 devices: a whole 2x2x4 slice. The times are simulated.
32 devices in a mesh: section: 4 (over x, core), blk: 8 (over z, y).
Axes of the slice: x: 2, y: 2, z: 4, core: 2. Of those that a mesh axis runs over, the one named last changes fastest.
Arguments:
- queries: bfloat16 [4, 1024, 4096], P('section', 'blk'), may hold values from -6 to 6
- key_heads: bfloat16 [4, 1024, 512], P('section', 'blk'), may hold values from -6 to 6
- value_per_head: bfloat16 [4, 1024, 512], P('section', 'blk'), may hold values from -6 to 6
- out_grads: bfloat16 [4, 1024, 4096], P('section', 'blk'), may hold values from -6 to 6
- segment_ids: int32 [4, 1024], P('section', 'blk'), may hold values from 0 to 63, never falling along the last dimension, each value on 1 to 64 neighbouring positions
- block_lists: int32 [4, 8, 4], P('section', 'blk'), may hold values from 0 to 7, as said below
- list_counts: int32 [4, 8], P('section', 'blk'), may hold values from 1 to 4, as said below
Outputs:
- grad_queries: bfloat16 [4, 1024, 4096], P('section', 'blk')
- grad_keys: bfloat16 [4, 1024, 512], P('section', 'blk')
- grad_values: bfloat16 [4, 1024, 512], P('section', 'blk')
Inputs may be any that keep to these rules, and one draw needn't show every extreme that they name: `block_lists`: entry 0 of row b is b itself; for b >= 1 entry 1 is block 0; entries 2 to list_counts - 1 are distinct blocks between 1 and b - 1; entries from list_counts on repeat b. `list_counts`: at least 2 for every query block after the first; the last query block of every micro-batch uses all 4 slots.
All inputs are finite; a program needn't handle non-finite values.
Results may differ from a plain program's by a relative error of at most 0.0051.
Values may be sent and summed in bfloat16 or wider, within the bound.
No kernel may reach another device: no remote copies, remote signals or barrier semaphores. Data moves between devices by JAX's collectives and lax.ppermute only.
A program may use at most 64 MiB of HBM per device.

v0:
```python
import math

import jax
import jax.numpy as jnp
from jax import lax
from jax.sharding import PartitionSpec as P

QUERY_HEADS = 32
KEY_VALUE_HEADS = 4
HEAD_SIZE = 128
MASK_BLOCK_SIZE = 128
LIST = 4


NEG_FILL = -1e30


def from_behind(value, axis, by):
    devices = lax.axis_size(axis)
    return lax.ppermute(value, axis, [(i, (i + by) % devices) for i in range(devices)])


def allowed_mask(block_ids, listed_count, query_block, query_segs):
    slot_ok = jnp.arange(LIST, dtype=jnp.int32) < listed_count
    own_block = block_ids == query_block
    positions = jnp.arange(MASK_BLOCK_SIZE, dtype=jnp.int32)
    causal = (positions[None, :] <= positions[:, None]) & (
        query_segs[None, :] == query_segs[:, None]
    )
    earlier = block_ids < query_block
    return slot_ok[None, :, None] & jnp.where(
        own_block[None, :, None], causal[:, None, :], earlier[None, :, None]
    )


def group_terms(query_row_slice, gradient_row_slice, key_rows, value_rows, allowed):
    scale_factor = 1.0 / math.sqrt(HEAD_SIZE)
    scores = (
        jnp.einsum("ihd,ljd->hilj", query_row_slice, key_rows, preferred_element_type=jnp.float32)
        * scale_factor
    )
    scores = jnp.where(allowed[None], scores, NEG_FILL)
    largest = jnp.max(scores, axis=(2, 3), keepdims=True)
    weights = jnp.where(allowed[None], jnp.exp(scores - largest), 0.0)
    probs_full = weights / jnp.sum(weights, axis=(2, 3), keepdims=True)
    dprobs = jnp.einsum(
        "ihd,ljd->hilj", gradient_row_slice, value_rows, preferred_element_type=jnp.float32
    )
    row_delta = jnp.sum(probs_full * dprobs, axis=(2, 3), keepdims=True)
    dscores = (probs_full * (dprobs - row_delta)).astype(jnp.bfloat16)
    probs_half = probs_full.astype(jnp.bfloat16)
    query_grad = (
        jnp.einsum("hilj,ljd->ihd", dscores, key_rows, preferred_element_type=jnp.float32)
        * scale_factor
    )
    key_grad = (
        jnp.einsum("hilj,ihd->ljd", dscores, query_row_slice, preferred_element_type=jnp.float32)
        * scale_factor
    )
    value_grad = jnp.einsum(
        "hilj,ihd->ljd", probs_half, gradient_row_slice, preferred_element_type=jnp.float32
    )
    return (query_grad, key_grad, value_grad)


def per_device(
    queries, key_heads, value_per_head, out_grads, segment_ids, block_lists, list_counts
):
    local_blocks = block_lists.shape[1]
    blk_count = lax.axis_size("blk")
    blocks_all = blk_count * local_blocks
    first_local = lax.axis_index("blk") * local_blocks
    heads_per_group = QUERY_HEADS // KEY_VALUE_HEADS
    key_value_width = KEY_VALUE_HEADS * HEAD_SIZE
    ids_all = block_lists[0]
    flat_ids = ids_all.reshape(-1)
    whole_keys, whole_values = (
        lax.all_gather(key_heads, "blk", axis=1, tiled=True),
        lax.all_gather(value_per_head, "blk", axis=1, tiled=True),
    )
    listed_k = whole_keys[0].reshape(blocks_all, MASK_BLOCK_SIZE, key_value_width)[flat_ids]
    listed_v = whole_values[0].reshape(blocks_all, MASK_BLOCK_SIZE, key_value_width)[flat_ids]
    query_all = queries[0]
    grads_all = out_grads[0]
    segs_all = segment_ids[0]
    counts_all = list_counts[0]
    query_block = first_local + 0
    row_hi = MASK_BLOCK_SIZE
    allowed = allowed_mask(ids_all[0], counts_all[0], query_block, segs_all)
    query_parts = []
    key_parts = []
    value_parts = []
    for shared_key_head in range(KEY_VALUE_HEADS):
        col_lo = shared_key_head * heads_per_group * HEAD_SIZE
        col_hi = col_lo + heads_per_group * HEAD_SIZE
        query_row_slice = query_all[0:row_hi, col_lo:col_hi].reshape(
            MASK_BLOCK_SIZE, heads_per_group, HEAD_SIZE
        )
        gradient_row_slice = grads_all[0:row_hi, col_lo:col_hi].reshape(
            MASK_BLOCK_SIZE, heads_per_group, HEAD_SIZE
        )
        head_keys = listed_k[:, :, shared_key_head * HEAD_SIZE : (shared_key_head + 1) * HEAD_SIZE]
        head_values = listed_v[
            :, :, shared_key_head * HEAD_SIZE : (shared_key_head + 1) * HEAD_SIZE
        ]
        query_grad, key_grad, value_grad = group_terms(
            query_row_slice, gradient_row_slice, head_keys, head_values, allowed
        )
        query_parts.append(query_grad.reshape(MASK_BLOCK_SIZE, heads_per_group * HEAD_SIZE))
        key_parts.append(key_grad)
        value_parts.append(value_grad)
    query_parts_all = jnp.concatenate(query_parts, axis=1).astype(jnp.bfloat16)
    grad_tiles = jnp.concatenate(key_parts + value_parts, axis=2)
    query_gradient_rows = query_parts_all[None]
    placement = (jnp.arange(blocks_all, dtype=jnp.int32)[:, None] == flat_ids[None, :]).astype(
        jnp.float32
    )
    term_all = jnp.einsum("cn,nrw->crw", placement, grad_tiles, precision=lax.Precision.HIGHEST)
    summed = lax.psum_scatter(
        term_all.reshape(blocks_all * MASK_BLOCK_SIZE, 2 * key_value_width),
        "blk",
        scatter_dimension=0,
        tiled=True,
    )
    summed_half = summed.astype(jnp.bfloat16)
    key_grads = summed_half[:, :key_value_width][None]
    value_grads = summed_half[:, key_value_width:][None]
    grad_queries, grad_keys, grad_values = from_behind(
        (query_gradient_rows, key_grads, value_grads), "section", -1
    )
    return (grad_queries, grad_keys, grad_values)


def solution(mesh):
    in_specs = (
        P("section", "blk", None),
        P("section", "blk", None),
        P("section", "blk", None),
        P("section", "blk", None),
        P("section", "blk"),
        P("section", "blk", None),
        P("section", "blk"),
    )
    out_specs = (P("section", "blk", None), P("section", "blk", None), P("section", "blk", None))
    return jax.shard_map(
        per_device, mesh=mesh, in_specs=in_specs, out_specs=out_specs, check_vma=False
    )
```

profile of v0, /device:TPU:1, one launch (start us, length us, event | category | flops | bytes accessed | tf_op | source)
XLA Modules:
  0.0 223.1 jit_solution(2614286710321186675)
XLA Ops:
  7.2 0.7 all-gather.3.cloned.1.call-update
  8.0 0.7 all-gather.5.cloned.1.call-update
  9.4 1.6 copy.22
  12.2 39.2 %all-gather.3.cloned.1.call-done = bf16[1,1024,512]{2,1,0:T(8,128)(2,1)} async-done(((bf16[1,128,512]{2,1,0:T(8,128)(2,1)}), bf16[1,1024,512]{2,1,0:T(8,128)(2,1)}) %all-gather.3.cloned.1.call-update) | async-done | bytes 1048592 | tf_op jit(solution)/shard_map/all_gather | solution.py:78
  51.4 1.8 gather_fusion
  53.2 39.3 %all-gather.5.cloned.1.call-done = bf16[1,1024,512]{2,1,0:T(8,128)(2,1)} async-done(((bf16[1,128,512]{2,1,0:T(8,128)(2,1)}), bf16[1,1024,512]{2,1,0:T(8,128)(2,1)}) %all-gather.5.cloned.1.call-update) | async-done | bytes 1048592 | tf_op jit(solution)/shard_map/all_gather | solution.py:79
  92.5 1.8 gather_fusion.1
  97.1 0.7 fusion.38
  97.8 1.7 fusion.9
  100.0 0.7 fusion.36
  100.7 1.8 fusion.6
  102.5 0.7 fusion.32
  103.2 0.7 fusion.34
  103.9 1.4 fusion.3
  105.3 2.4 %fusion.11 = (bf16[8,128,4,128]{1,3,0,2:T(8,128)(2,1)S(1)}, bf16[8,128,4,128]{1,3,0,2:T(8,128)(2,1)S(1)}, bf16[8,128,4,128]{1,3,0,2:T(8,128)(2,1)S(1)}) fusion(f32[4,128,128,8]{2,1,3,0:T(8,128)S(1)} %get-tuple-element.29, f32[8,128]{1,0:T(8,128)S(1)} %get-tuple-element.3, f32[8,128]{1,0:T(8,128)S(1)} %fusion.17, f32[8,128]{1,0:T(8,128)S(1)} %get-tuple-element.27, ...), kind=kLoop, calls=%fused_computation.24 | loop fusion | flops 12582912 | bytes 15831040 | tf_op jit(solution)/shard_map/convert_element_type | solution.py:50
  109.1 0.7 fusion.5
  112.3 2.6 %fusion.54 = f32[8,128,1024]{2,0,1:T(8,128)S(1)} fusion(f32[4,128,1024]{2,0,1:T(4,128)S(1)} %bitcast_dynamic-update-slice_fusion, s32[4]{0:T(128)S(1)} %bitcast.344), kind=kOutput, calls=%fused_computation.100 | convolution fusion | flops 50331680 | bytes 6291472 | tf_op jit(solution)/shard_map/cn,nrw->crw/dot_general | solution.py:118
  114.9 4.4 %copy.44 = f32[8,128,1024]{2,1,0:T(8,128)} copy(f32[8,128,1024]{2,0,1:T(8,128)S(1)} %fusion.54) | data formatting | bytes 8388608 | tf_op jit(solution)/shard_map/cn,nrw->crw/dot_general | solution.py:118
  119.3 1.2 fusion.31
  120.5 0.9 copy.40
  121.4 1.2 fusion.28
  122.7 0.9 copy.43
  123.5 1.3 fusion.29
  125.0 1.2 fusion.30
  126.5 1.7 collective-permute-start
  128.2 79.1 %reduce-scatter.2.cloned.1.call-done = f32[128,1024]{1,0:T(8,128)} async-done(((f32[1024,1024]{1,0:T(8,128)}), f32[128,1024]{1,0:T(8,128)}) %reduce-scatter.2.cloned.1.call-update) | async-done | bytes 524304 | tf_op jit(solution)/shard_map/reduce_scatter | solution.py:119
  207.3 1.1 convert_element_type.44
  208.4 0.7 collective-permute-start.2
  209.1 0.9 collective-permute-start.1
  210.1 2.8 %collective-permute-done.2 = bf16[1,128,512]{2,1,0:T(8,128)(2,1)S(1)} collective-permute-done((bf16[1,128,512]{2,1,0:T(8,128)(2,1)S(1)}, bf16[1,128,512]{2,1,0:T(8,128)(2,1)S(1)}, u32[]{:S(2)}, u32[]{:S(2)}) %collective-permute-start.2) | collective-permute-done | bytes 131104 | tf_op jit(solution)/shard_map/ppermute | solution.py:20
  212.9 1.4 collective-permute-done.1
  214.3 1.0 copy.116
  (67 shorter events, 9.8 us)
Async XLA Ops:
  7.2 3.8 %copy-start.9 = (bf16[1,128,4096]{2,1,0:T(8,128)(2,1)S(1)}, bf16[1,128,4096]{2,1,0:T(8,128)(2,1)}, u32[]{:S(2)}) copy-start(bf16[1,128,4096]{2,1,0:T(8,128)(2,1)} %param.10) | copy-start | bytes 3145732
  7.2 44.2 %all-gather.3.cloned.1.call-start = ((), (), s32[]{:S(2)}) async-start(), calls=%async_computation.1 | async-start | bytes 1179648 | tf_op jit(solution)/shard_map/all_gather | solution.py:78
  7.9 84.6 %all-gather.5.cloned.1.call-start = ((), (), s32[]{:S(2)}) async-start(), calls=%async_computation.2 | async-start | bytes 1179648 | tf_op jit(solution)/shard_map/all_gather | solution.py:79
  8.7 198.7 %reduce-scatter.2.cloned.1.call-start = ((), (), s32[]{:S(2)}) async-start(), calls=%async_computation.3 | async-start | bytes 4718592 | tf_op jit(solution)/shard_map/reduce_scatter | solution.py:119
  9.4 2.3 %copy-start.12 = (s32[1,1,4]{2,1,0:T(1,128)S(1)}, s32[1,1,4]{2,1,0:T(1,128)}, u32[]{:S(2)}) copy-start(s32[1,1,4]{2,1,0:T(1,128)} %param.12) | copy-start | bytes 52
  9.4 2.4 %copy-start.13 = (s32[1,128]{1,0:T(1,128)S(1)}, s32[1,128]{1,0:T(1,128)}, u32[]{:S(2)}) copy-start(s32[1,128]{1,0:T(1,128)} %param.11) | copy-start | bytes 1540
  12.0 82.7 %copy-start.5 = (bf16[128,1024]{0,1:T(8,128)(2,1)}, bf16[128,1024]{0,1:T(8,128)(2,1)S(1)}, u32[]{:S(2)}) copy-start(bf16[128,1024]{0,1:T(8,128)(2,1)S(1)} %get-tuple-element.12) | copy-start | bytes 786436
  12.1 83.2 %copy-start.3 = (bf16[128,1024]{0,1:T(8,128)(2,1)}, bf16[128,1024]{0,1:T(8,128)(2,1)S(1)}, u32[]{:S(2)}) copy-start(bf16[128,1024]{0,1:T(8,128)(2,1)S(1)} %get-tuple-element.14) | copy-start | bytes 786436
  12.1 84.0 %copy-start.7 = (bf16[128,1024]{0,1:T(8,128)(2,1)}, bf16[128,1024]{0,1:T(8,128)(2,1)S(1)}, u32[]{:S(2)}) copy-start(bf16[128,1024]{0,1:T(8,128)(2,1)S(1)} %get-tuple-element.15) | copy-start | bytes 786436
  53.2 42.9 %copy-start.2 = (bf16[4,128,512]{2,1,0:T(8,128)(2,1)}, bf16[4,128,512]{2,1,0:T(8,128)(2,1)S(1)}, u32[]{:S(2)}) copy-start(bf16[4,128,512]{2,1,0:T(8,128)(2,1)S(1)} %gather_fusion) | copy-start | bytes 1572868
  105.3 2.5 %copy-start.8 = (bf16[128,1024]{0,1:T(8,128)(2,1)S(1)}, bf16[128,1024]{0,1:T(8,128)(2,1)}, u32[]{:S(2)}) copy-start(bf16[128,1024]{0,1:T(8,128)(2,1)} %copy-done.7) | copy-start | bytes 786436
  105.3 2.9 %copy-start.6 = (bf16[128,1024]{0,1:T(8,128)(2,1)S(1)}, bf16[128,1024]{0,1:T(8,128)(2,1)}, u32[]{:S(2)}) copy-start(bf16[128,1024]{0,1:T(8,128)(2,1)} %copy-done.5) | copy-start | bytes 786436
  107.7 1.0 copy-start.4
  109.8 1.7 copy-start
  120.5 3.0 %copy-start.1 = (bf16[8,128,4,128]{1,3,0,2:T(8,128)(2,1)S(1)}, bf16[8,128,4,128]{1,3,0,2:T(8,128)(2,1)}, u32[]{:S(2)}) copy-start(bf16[8,128,4,128]{1,3,0,2:T(8,128)(2,1)} %copy-done) | copy-start | bytes 3145732
  123.5 2.8 %copy-start.10 = (bf16[1,128,1024]{2,1,0:T(8,128)(2,1)S(1)}, bf16[1,128,1024]{2,1,0:T(8,128)(2,1)}, u32[]{:S(2)}) copy-start(bf16[1,128,1024]{2,1,0:T(8,128)(2,1)} %copy.40) | copy-start | bytes 786436
  124.8 1.6 copy-start.11
  126.5 83.6 %collective-permute-start = (bf16[1,128,4096]{2,1,0:T(8,128)(2,1)S(1)}, bf16[1,128,4096]{2,1,0:T(8,128)(2,1)S(1)}, u32[]{:S(2)}, u32[]{:S(2)}) collective-permute-start(bf16[1,128,4096]{2,1,0:T(8,128)(2,1)S(1)} %pad_maximum_fusion), channel_id=1, source_target_pairs={{0,24},{8,0},{16,8},{24,16},{1,25},{9,1},{17,9},{25,17},{2,26},{10... | collective-permute-start | bytes 3145736 | tf_op jit(solution)/shard_map/ppermute | solution.py:20
  208.4 4.4 %collective-permute-start.2 = (bf16[1,128,512]{2,1,0:T(8,128)(2,1)S(1)}, bf16[1,128,512]{2,1,0:T(8,128)(2,1)S(1)}, u32[]{:S(2)}, u32[]{:S(2)}) collective-permute-start(bf16[1,128,512]{2,1,0:T(8,128)(2,1)S(1)} %get-tuple-element.20), channel_id=1, source_target_pairs={{0,24},{8,0},{16,8},{24,16},{1,25},{9,1},{17,9},{25,17},{2,26},{10... | collective-permute-start | bytes 393224 | tf_op jit(solution)/shard_map/ppermute | solution.py:20
  209.1 5.2 %collective-permute-start.1 = (bf16[1,128,512]{2,1,0:T(8,128)(2,1)S(1)}, bf16[1,128,512]{2,1,0:T(8,128)(2,1)S(1)}, u32[]{:S(2)}, u32[]{:S(2)}) collective-permute-start(bf16[1,128,512]{2,1,0:T(8,128)(2,1)S(1)} %get-tuple-element.21), channel_id=1, source_target_pairs={{0,24},{8,0},{16,8},{24,16},{1,25},{9,1},{17,9},{25,17},{2,26},{10... | collective-permute-start | bytes 393224 | tf_op jit(solution)/shard_map/ppermute | solution.py:20
Sparse Core Ops, SparseCore 0:
  10.1 41.2 all-gather.2
  53.5 38.9 all-gather.4
  119.4 87.8 reduce-scatter.1
where the time goes:
time: 223 us
  waiting for transfers between devices  163 us (73%)
  matrix products  19.1 us (9%)
  local copies, waits for them, and re-layouts  15.8 us (7%)
  between operations  14.9 us (7%)
  other arithmetic  6.55 us (3%)
  starting transfers between devices  3.5 us (2%)
    reduce_scatter x1, waiting for transfers between devices, per_device(): lax.psum_scatter(term_all.reshape(blocks_all * MASK_BLOCK_SIZE, 2 * key_v...  79.1 us
    all_gather x1, waiting for transfers between devices, per_device(): lax.all_gather(value_per_head, 'blk', axis=1, tiled=True)  39.3 us
    all_gather x1, waiting for transfers between devices, per_device(): lax.all_gather(key_heads, 'blk', axis=1, tiled=True)  39.2 us
    unnamed x36, local copies, waits for them, and re-layouts  5.38 us
    dot_general x4, matrix products, group_terms(): jnp.einsum('ihd,ljd->hilj', gradient_row_slice, value_rows, preferred_ele...  5.29 us
    dot_general x4, matrix products, group_terms(): jnp.einsum('hilj,ljd->ihd', dscores, key_rows, preferred_element_type=jnp...  4.99 us
  transfers between devices with their start and end apart: 6, of which 5 were waited for; matrix products, arithmetic and copies ran while one was open for 6% of the time, Pallas kernels for 0%

commit v1 on v0

v1 whole, which is shorter than its diff:
```python
import math

import jax
import jax.numpy as jnp
from jax import lax
from jax.experimental import pallas as pl
from jax.experimental.pallas import tpu as pltpu
from jax.sharding import PartitionSpec as P

QUERY_HEADS = 32
KEY_VALUE_HEADS = 4
HEAD_SIZE = 128
BLOCK = 128
LIST = 4
GROUP = QUERY_HEADS // KEY_VALUE_HEADS
HALF_KV = KEY_VALUE_HEADS // 2
HALF_Q = QUERY_HEADS // 2 * HEAD_SIZE
KV_COLS = HALF_KV * HEAD_SIZE
WIDE = GROUP * HEAD_SIZE
PAIR = 2 * HEAD_SIZE
MASKED = -1e30
NONE, WHOLE, CAUSAL = 0, 1, 2

SCALE = 1.0 / math.sqrt(HEAD_SIZE)
LOG2E = 1.0 / math.log(2.0)


def dot(a, b, contract):
    return lax.dot_general(
        a, b, ((contract[0], contract[1]), ((), ())), preferred_element_type=jnp.float32
    )


def attention_kernel(levels, *refs):
    place_ref, mode_ref, side_ref, segs_ref = refs[:4]
    query_ref, grad_ref, partner_ref = refs[4:7]
    held = refs[7 : 7 + levels]
    own_out, partner_out, here_ref = refs[7 + levels : 10 + levels]
    away_refs = refs[10 + levels : 9 + 2 * levels]
    kv, near, far, bias, probs, dscores, sums, arrived = refs[-8:]

    first_col = pl.multiple_of(side_ref[0] * HALF_Q, HALF_Q)
    copies = [
        pltpu.make_async_copy(held[j], kv.at[pl.ds(2 * j * BLOCK, 2 * BLOCK)], arrived.at[j])
        for j in range(levels)
    ]
    for which, ref in enumerate((query_ref, grad_ref)):
        copies.append(
            pltpu.make_async_copy(
                ref.at[:, pl.ds(first_col, HALF_Q)], near.at[which], arrived.at[levels + which]
            )
        )
    late = pltpu.make_async_copy(partner_ref, far, arrived.at[levels + 2])
    for copy in copies:
        copy.start()
    late.start()
    sums[...] = jnp.zeros_like(sums)

    key_at = lax.broadcasted_iota(jnp.int32, (BLOCK, BLOCK), 0)
    query_at = lax.broadcasted_iota(jnp.int32, (BLOCK, BLOCK), 1)
    for block in range(2):
        seg_of_query = jnp.broadcast_to(segs_ref[block : block + 1, :], (BLOCK, BLOCK))
        seg_of_key = seg_of_query.T
        causal = (key_at <= query_at) & (seg_of_key == seg_of_query)
        causal_bias = jnp.where(causal, 0.0, MASKED)
        for slot in range(LIST):
            mode = mode_ref[block * LIST + slot]
            flat = jnp.where(mode == WHOLE, 0.0, MASKED)
            bias[slot * BLOCK : (slot + 1) * BLOCK, :] = jnp.where(
                mode == CAUSAL, causal_bias, flat
            )
        if block == 0:
            for copy in copies:
                copy.wait()
        else:
            late.wait()

        def rows(which, head):
            if block == 0:
                return near[which, :, head * HEAD_SIZE : (head + 1) * HEAD_SIZE]
            start = which * HALF_Q + head * HEAD_SIZE
            return far[:, start : start + HEAD_SIZE]

        out = (own_out, partner_out)[block]
        places = [
            pl.ds(pl.multiple_of(place_ref[block * LIST + slot] * BLOCK, BLOCK), BLOCK)
            for slot in range(LIST)
        ]
        for group in range(HALF_KV):
            key_cols = slice(group * PAIR, group * PAIR + HEAD_SIZE)
            value_cols = slice(group * PAIR + HEAD_SIZE, (group + 1) * PAIR)
            heads = [group * GROUP + h for h in range(GROUP)]
            keys = jnp.concatenate([kv[at, key_cols] for at in places], axis=0)
            values = jnp.concatenate([kv[at, value_cols] for at in places], axis=0)
            for h in range(0, GROUP, 2):
                query = jnp.concatenate([rows(0, heads[h]), rows(0, heads[h + 1])], axis=0)
                grad = jnp.concatenate([rows(1, heads[h]), rows(1, heads[h + 1])], axis=0)
                scores = dot(keys, query, ((1,), (1,)))
                fill = jnp.concatenate([bias[...], bias[...]], axis=1)
                scores = scores * (SCALE * LOG2E) + fill
                weights = jnp.exp2(scores - jnp.max(scores, axis=0, keepdims=True))
                inverse = 1.0 / jnp.sum(weights, axis=0, keepdims=True)
                dprobs = dot(values, grad, ((1,), (1,)))
                full = weights * inverse
                delta = jnp.sum(full * dprobs, axis=0, keepdims=True)
                at = slice(h * BLOCK, (h + 2) * BLOCK)
                probs[:, at] = full.astype(jnp.bfloat16)
                dscores[:, at] = (full * (dprobs - delta)).astype(jnp.bfloat16)
            query_all = jnp.concatenate([rows(0, head) for head in heads], axis=0)
            grad_all = jnp.concatenate([rows(1, head) for head in heads], axis=0)
            key_terms = dot(dscores[...], query_all, ((1,), (0,))) * SCALE
            value_terms = dot(probs[...], grad_all, ((1,), (0,)))
            for slot in range(LIST):
                at = slice(slot * BLOCK, (slot + 1) * BLOCK)
                sums[places[slot], key_cols] += key_terms[at]
                sums[places[slot], value_cols] += value_terms[at]
            for h, head in enumerate(heads):
                query_grad = dot(dscores[:, h * BLOCK : (h + 1) * BLOCK], keys, ((0,), (0,)))
                out[:, head * HEAD_SIZE : (head + 1) * HEAD_SIZE] = (query_grad * SCALE).astype(
                    jnp.bfloat16
                )
    here_ref[...] = sums[: 2 * BLOCK]
    for j, ref in enumerate(away_refs):
        ref[...] = sums[2 * (j + 1) * BLOCK : 2 * (j + 2) * BLOCK].astype(ref.dtype)


def attention(levels, place, mode, side, segs, queries, grads, partner, held):
    smem = pl.BlockSpec(memory_space=pltpu.SMEM)
    vmem = pl.BlockSpec(memory_space=pltpu.VMEM)
    keys = LIST * BLOCK
    width = HALF_KV * PAIR
    outs = [
        jax.ShapeDtypeStruct((BLOCK, HALF_Q), jnp.bfloat16),
        jax.ShapeDtypeStruct((BLOCK, HALF_Q), jnp.bfloat16),
        jax.ShapeDtypeStruct((2 * BLOCK, width), jnp.float32),
    ]
    for j in range(1, levels):
        kind = jnp.float32 if 1 < j < levels - 1 else jnp.bfloat16
        outs.append(jax.ShapeDtypeStruct((2 * BLOCK, width), kind))
    return pl.pallas_call(
        lambda *refs: attention_kernel(levels, *refs),
        out_shape=outs,
        in_specs=[smem, smem, smem, vmem] + [pl.BlockSpec(memory_space=pl.ANY)] * (3 + levels),
        out_specs=[vmem] * len(outs),
        scratch_shapes=[
            pltpu.VMEM((2 * levels * BLOCK, width), jnp.bfloat16),
            pltpu.VMEM((2, BLOCK, HALF_Q), jnp.bfloat16),
            pltpu.VMEM((BLOCK, 2 * HALF_Q), jnp.bfloat16),
            pltpu.VMEM((keys, BLOCK), jnp.float32),
            pltpu.VMEM((keys, WIDE), jnp.bfloat16),
            pltpu.VMEM((keys, WIDE), jnp.bfloat16),
            pltpu.VMEM((2 * levels * BLOCK, width), jnp.float32),
            pltpu.SemaphoreType.DMA((levels + 3,)),
        ],
        compiler_params=pltpu.CompilerParams(vmem_limit_bytes=60 * 1024 * 1024),
        cost_estimate=pl.CostEstimate(
            flops=5 * 2 * keys * HEAD_SIZE * BLOCK * QUERY_HEADS,
            bytes_accessed=8 * 1024 * 1024,
            transcendentals=keys * BLOCK * QUERY_HEADS,
        ),
    )(place, mode, side, segs, queries, grads, partner, *held)


def per_device(
    queries, key_heads, value_per_head, out_grads, segment_ids, block_lists, list_counts
):
    sections = lax.axis_size("section")
    blocks = lax.axis_size("blk")
    levels = blocks // 2
    mine = lax.axis_index("blk")
    side = mine % 2
    level = mine // 2
    swap = [(i, i ^ 1) for i in range(blocks)]

    def back(value, moved):
        pairs = [
            (s * blocks + b, (s - 1) % sections * blocks + moved(b))
            for s in range(sections)
            for b in range(blocks)
            if moved(b) >= 0
        ]
        return lax.ppermute(value, ("section", "blk"), pairs)

    def columns(array, start, width):
        return lax.dynamic_slice_in_dim(array[0], start, width, 1)

    def heads_of(half):
        parts = []
        for g in range(HALF_KV):
            start = half * KV_COLS + g * HEAD_SIZE
            parts += [columns(a, start, HEAD_SIZE) for a in (key_heads, value_per_head)]
        return jnp.concatenate(parts, axis=1)

    facts = jnp.concatenate([segment_ids[0], block_lists[0, 0], list_counts[0]])[None]
    facts_got = lax.ppermute(facts, "blk", swap)
    other = lax.ppermute(heads_of(1 - side), "blk", swap)
    theirs = jnp.concatenate(
        [columns(a, (1 - side) * HALF_Q, HALF_Q) for a in (queries, out_grads)], axis=1
    )
    theirs, other, facts_got = lax.optimization_barrier((theirs, other, facts_got))
    partner = lax.ppermute(theirs, "blk", swap)
    held = [jnp.concatenate([heads_of(side), other], axis=0)]
    for hop in range(1, levels):
        pairs = [(i, i + 2 * hop) for i in range(blocks - 2 * hop)]
        held.append(lax.ppermute(held[0], "blk", pairs))

    facts = jnp.concatenate([facts, facts_got], axis=0)
    segs = facts[:, :BLOCK]
    lists = facts[:, BLOCK : BLOCK + LIST]
    counts = facts[:, BLOCK + LIST :]
    block = jnp.stack([mine, mine ^ 1])[:, None].astype(jnp.int32)
    listed = jnp.arange(LIST, dtype=jnp.int32)[None, :] < counts
    mode = jnp.where(lists == block, CAUSAL, jnp.where(lists < block, WHOLE, NONE))
    mode = jnp.where(listed, mode, NONE).astype(jnp.int32)
    place = 2 * (level - lists // 2) + (lists % 2 != side).astype(jnp.int32)
    place = jnp.where(mode == NONE, 0, place).astype(jnp.int32)

    own_out, partner_out, here, *away = attention(
        levels,
        place.reshape(-1),
        mode.reshape(-1),
        side.astype(jnp.int32)[None],
        segs,
        queries[0],
        out_grads[0],
        partner,
        held,
    )
    query_grads = (back(own_out, lambda b: b), back(partner_out, lambda b: b ^ 1))

    def down(terms, hop):
        return lax.ppermute(terms, "blk", [(i, i - 2 * hop) for i in range(2 * hop, blocks)])

    landed = []
    if levels > 1:
        landed.append(down(away[0], 1))
    if levels > 2:
        total = away[-1]
        for j in range(levels - 2, 1, -1):
            pairs = [(i, i - 2) for i in range(2 * (j + 1), blocks)]
            carried = lax.ppermute(total, "blk", pairs)
            total = (away[j - 1].astype(jnp.float32) + carried.astype(jnp.float32)).astype(jnp.bfloat16)
        landed.append(down(total, 2))
    landed, query_grads = lax.optimization_barrier((landed, query_grads))
    for terms in landed:
        here = here + terms.astype(jnp.float32)
    totals = here.astype(jnp.bfloat16)
    sums = [back(totals[:BLOCK], lambda b: b), back(totals[BLOCK:], lambda b: b ^ 1)]

    def ordered(a, b):
        return jnp.where(side == 0, jnp.concatenate([a, b], axis=1), jnp.concatenate([b, a], axis=1))

    grad_queries = ordered(*query_grads)

    def kind(total, which):
        starts = [g * PAIR + which * HEAD_SIZE for g in range(HALF_KV)]
        return jnp.concatenate([total[:, at : at + HEAD_SIZE] for at in starts], axis=1)

    grad_keys = ordered(kind(sums[0], 0), kind(sums[1], 0))
    grad_values = ordered(kind(sums[0], 1), kind(sums[1], 1))
    return (grad_queries[None], grad_keys[None], grad_values[None])


def solution(mesh):
    in_specs = (
        P("section", "blk", None),
        P("section", "blk", None),
        P("section", "blk", None),
        P("section", "blk", None),
        P("section", "blk"),
        P("section", "blk", None),
        P("section", "blk"),
    )
    out_specs = (P("section", "blk", None), P("section", "blk", None), P("section", "blk", None))
    return jax.shard_map(
        per_device, mesh=mesh, in_specs=in_specs, out_specs=out_specs, check_vma=False
    )
```

time: 223 us -> 81.4 us (0.37)
  waiting for transfers between devices: 163 us -> 36 us
  matrix products: 19.1 us -> 0 us
  starting transfers between devices: 3.5 us -> 20.4 us
  between operations: 14.9 us -> 1.49 us
  Pallas kernels: 0 us -> 13 us
  local copies, waits for them, and re-layouts: 15.8 us -> 4.52 us
    reduce_scatter x1 -> x0, waiting for transfers between devices: 79.1 us -> none  [per_device(): lax.psum_scatter(term_all.reshape(blocks_all * MASK_BLOCK_SIZE, 2 * key_v...]
    all_gather x2 -> x0, waiting for transfers between devices: 78.6 us -> none  [the longest x1 39.3 us: per_device(): lax.all_gather(value_per_head, 'blk', axis=1, tiled=True)]
    ppermute x3 -> x13, waiting for transfers between devices: 4.21 us -> 36 us  [the longest x2 19.3 us: down(): lax.ppermute(terms, 'blk', [(i, i - 2 * hop) for i in range(2 * hop, bloc...]
    dot_general x21 -> x0, matrix products: 19.1 us -> none  [the longest x4 5.29 us: group_terms(): jnp.einsum('ihd,ljd->hilj', gradient_row_slice, value_rows, preferred_ele...]
    ppermute x3 -> x13, starting transfers between devices: 3.39 us -> 20.4 us  [the longest x3 8.74 us: per_device(): held.append(lax.ppermute(held[0], 'blk', pairs))]
    pallas_call x0 -> x1, Pallas kernels: none -> 13 us  [attention(): pl.pallas_call(lambda *refs: attention_kernel(levels, *refs), out_shape=o...]
    unnamed x36 -> x12, local copies, waits for them, and re-layouts: 5.38 us -> 0.97 us
    dot_general x1 -> x0, local copies, waits for them, and re-layouts: 4.36 us -> none  [per_device(): jnp.einsum('cn,nrw->crw', placement, grad_tiles, precision=lax.Precision....]
  transfers between devices with their start and end apart: 6 -> 13, of which waited for: 5 -> 8; matrix products, arithmetic and copies ran while one was open for 6% -> 8% of each run, Pallas kernels for 0% -> 0%
where the time goes in v1:
time: 81.4 us; the launch traced here: 80.9 us
  waiting for transfers between devices  36 us (44%)
  starting transfers between devices  20.4 us (25%)
  Pallas kernels  13 us (16%)
  other arithmetic  5.58 us (7%)
  local copies, waits for them, and re-layouts  4.52 us (6%)
  between operations  1.49 us (2%)
    ppermute x2, waiting for transfers between devices, down(): lax.ppermute(terms, 'blk', [(i, i - 2 * hop) for i in range(2 * hop, bloc...  19.3 us
    pallas_call x1, Pallas kernels, attention(): pl.pallas_call(lambda *refs: attention_kernel(levels, *refs), out_shape=o...  13 us
    ppermute x3, starting transfers between devices, per_device(): held.append(lax.ppermute(held[0], 'blk', pairs))  8.74 us
    ppermute x3, waiting for transfers between devices, per_device(): held.append(lax.ppermute(held[0], 'blk', pairs))  8.25 us
    ppermute x4, starting transfers between devices, back(): return lax.ppermute(value, ('section', 'blk'), pairs)  5.79 us
    ppermute x4, waiting for transfers between devices, back(): return lax.ppermute(value, ('section', 'blk'), pairs)  3.9 us
    ppermute x1, waiting for transfers between devices, per_device(): partner = lax.ppermute(theirs, 'blk', swap)  3.21 us
    select_n x3, other arithmetic, ordered(): jnp.where(side == 0, jnp.concatenate([a, b], axis=1), jnp.concatenate([b,...  2.59 us
  transfers between devices with their start and end apart: 13, of which 8 were waited for; matrix products, arithmetic and copies ran while one was open for 8% of the time, Pallas kernels for 0%

profile of v1, /device:TPU:1, one launch (start us, length us, event | category | flops | bytes accessed | tf_op | source)
XLA Modules:
  0.0 80.9 jit_solution(4951390383746166961)
XLA Ops:
  0.7 0.9 %dynamic-slice_bitcast_fusion.4 = (bf16[128,128]{1,0:T(8,128)(2,1)S(1)}, bf16[128,128]{1,0:T(8,128)(2,1)S(1)}, bf16[128,128]{1,0:T(8,128)(2,1)S(1)}, bf16[128,12...) fusion(bf16[1,128,512]{2,1,0:T(8,128)(2,1)} %param.9, ...), kind=kLoop, calls=%fused_computation.20 | loop fusion | bytes 524304 | tf_op jit(solution)/shard_map/dynamic_slice | solution.py:185
  1.6 2.1 %collective-permute-start = (bf16[128,512]{1,0:T(8,128)(2,1)S(1)}, bf16[128,512]{1,0:T(8,128)(2,1)S(1)}, u32[]{:S(2)}, u32[]{:S(2)}) collective-permute-start(bf16[128,512]{1,0:T(8,128)(2,1)S(1)} %pad_maximum_fusion.2), channel_id=1, source_target_pairs={{0,1},{1,0},{2,3},{3,2},{4,5},{5,4},{6,7},{7,6},{8,9},{9,8},{10,11... | collective-permute-start | bytes 393224 | tf_op jit(solution)/shard_map/ppermute | solution.py:196
  4.4 0.7 pad_add_fusion.1
  5.1 1.3 %dynamic-slice_bitcast_fusion = (bf16[128,2048]{1,0:T(8,128)(2,1)S(1)}, bf16[128,2048]{1,0:T(8,128)(2,1)S(1)}) fusion(bf16[1,128,4096]{2,1,0:T(8,128)(2,1)} %param.10, s32[]{:T(128)S(6)} %select_n.101, bf16[1,128,4096]{2,1,0:T(8,128)(2,1)} %param.7), kind=kLoop, calls=%fused_computation.4 | loop fusion | bytes 2097156 | tf_op jit(solution)/shard_map/dynamic_slice | solution.py:185
  6.5 1.3 %collective-permute-done.1 = s32[1,133]{1,0:T(1,128)S(1)} collective-permute-done((s32[1,133]{1,0:T(1,128)S(1)}, s32[1,133]{1,0:T(1,128)S(1)}, u32[]{:S(2)}, u32[]{:S(2)}) %collective-permute-start.1) | collective-permute-done | bytes 564 | tf_op jit(solution)/shard_map/ppermute | solution.py:195
  7.8 0.3 collective-permute-start.2
  8.2 3.2 %collective-permute-start.3 = (bf16[256,512]{1,0:T(8,128)(2,1)S(1)}, bf16[256,512]{1,0:T(8,128)(2,1)S(1)}, u32[]{:S(2)}, u32[]{:S(2)}) collective-permute-start(bf16[256,512]{1,0:T(8,128)(2,1)S(1)} %pad_maximum_fusion.1.refs_7_), channel_id=1, source_target_pairs={{0,2},{1,3},{2,4},{3,5},{4,6},{5,7},{8,10},{9,11},{10,12},{11,13},... | collective-permute-start | bytes 786440 | tf_op jit(solution)/shard_map/ppermute | solution.py:205
  11.5 4.2 %collective-permute-start.4 = (bf16[256,512]{1,0:T(8,128)(2,1)S(1)}, bf16[256,512]{1,0:T(8,128)(2,1)S(1)}, u32[]{:S(2)}, u32[]{:S(2)}) collective-permute-start(bf16[256,512]{1,0:T(8,128)(2,1)S(1)} %pad_maximum_fusion.1.refs_7_), channel_id=1, source_target_pairs={{0,4},{1,5},{2,6},{3,7},{8,12},{9,13},{10,14},{11,15},{16,20},{17,... | collective-permute-start | bytes 786440 | tf_op jit(solution)/shard_map/ppermute | solution.py:205
  15.7 1.3 %collective-permute-start.5 = (bf16[256,512]{1,0:T(8,128)(2,1)S(1)}, bf16[256,512]{1,0:T(8,128)(2,1)S(1)}, u32[]{:S(2)}, u32[]{:S(2)}) collective-permute-start(bf16[256,512]{1,0:T(8,128)(2,1)S(1)} %pad_maximum_fusion.1.refs_7_), channel_id=1, source_target_pairs={{0,6},{1,7},{8,14},{9,15},{16,22},{17,23},{24,30},{25,31}} | collective-permute-start | bytes 786440 | tf_op jit(solution)/shard_map/ppermute | solution.py:205
  17.0 0.2 fusion.3
  17.3 0.7 reshape.292.refs_0_
  17.9 0.6 reshape.293.refs_1_
  18.5 0.6 pad_add_fusion.refs_3_
  19.1 2.6 %collective-permute-done.4.refs_9_ = bf16[256,512]{1,0:T(8,128)(2,1)S(1)} collective-permute-done((bf16[256,512]{1,0:T(8,128)(2,1)S(1)}, bf16[256,512]{1,0:T(8,128)(2,1)S(1)}, u32[]{:S(2)}, u32[]{:S(2)}) %collective-permute-start.4) | collective-permute-done | bytes 262176 | tf_op jit(solution)/shard_map/ppermute | solution.py:205
  21.8 5.6 %collective-permute-done.5.refs_10_ = bf16[256,512]{1,0:T(8,128)(2,1)S(1)} collective-permute-done((bf16[256,512]{1,0:T(8,128)(2,1)S(1)}, bf16[256,512]{1,0:T(8,128)(2,1)S(1)}, u32[]{:S(2)}, u32[]{:S(2)}) %collective-permute-start.5) | collective-permute-done | bytes 262176 | tf_op jit(solution)/shard_map/ppermute | solution.py:205
  27.4 3.2 %collective-permute-done.2.refs_6_ = bf16[128,4096]{1,0:T(8,128)(2,1)S(1)} collective-permute-done((bf16[128,4096]{1,0:T(8,128)(2,1)S(1)}, bf16[128,4096]{1,0:T(8,128)(2,1)S(1)}, u32[]{:S(2)}, u32[]{:S(2)}) %collective-permute-start.2) | collective-permute-done | bytes 1048608 | tf_op jit(solution)/shard_map/ppermute | solution.py:201
  30.6 0.9 %copy-done.2 = bf16[128,4096]{1,0:T(8,128)(2,1)} copy-done((bf16[128,4096]{1,0:T(8,128)(2,1)}, bf16[128,4096]{1,0:T(8,128)(2,1)S(1)}, u32[]{:S(2)}) %copy-start.2) | copy-done | bytes 1048600
  31.6 13.0 %shard_map.94 = (bf16[128,2048]{1,0:T(8,128)(2,1)}, bf16[128,2048]{1,0:T(8,128)(2,1)}, f32[256,512]{1,0:T(8,128)}, bf16[256,512]{1,0:T(8,128)(2,1)}, f32[256,512]{1,0:T(8,128)}, /*index=5*/bf16[256,512]{1,0:T(8,128)(2,1)}) custom-call(s32[8]{0:T(128)} %reshape.292.refs_0_, s32[8]{0:T(128)} %reshape.293.refs_1_, s32[1]{0:T(128)} %bitcast.12.refs_2_, ...), custom_call_target="tpu_custom_call" | custom-call | flops 2684354560 | bytes 8388608 | tf_op jit(solution)/shard_map/pallas_call | solution.py:140
  44.6 0.8 collective-permute-start.7
  45.4 3.1 %collective-permute-start.10 = (bf16[128,2048]{1,0:T(8,128)(2,1)}, bf16[128,2048]{1,0:T(8,128)(2,1)S(1)}, u32[]{:S(2)}, u32[]{:S(2)}) collective-permute-start(bf16[128,2048]{1,0:T(8,128)(2,1)} %get-tuple-element.23), channel_id=1, source_target_pairs={{0,25},{1,24},{2,27},{3,26},{4,29},{5,28},{6,31},{7,30},{8,1},{9,0... | collective-permute-start | bytes 1572872 | tf_op jit(solution)/shard_map/ppermute | solution.py:182
  48.5 1.3 %collective-permute-start.6 = (bf16[256,512]{1,0:T(8,128)(2,1)}, bf16[256,512]{1,0:T(8,128)(2,1)S(1)}, u32[]{:S(2)}, u32[]{:S(2)}) collective-permute-start(bf16[256,512]{1,0:T(8,128)(2,1)} %get-tuple-element.19), channel_id=1, source_target_pairs={{2,0},{3,1},{4,2},{5,3},{6,4},{7,5},{10,8},{11,9},{12,10},{13,11},... | collective-permute-start | bytes 786440 | tf_op jit(solution)/shard_map/ppermute | solution.py:232
  49.8 1.1 %add_convert_fusion.1 = bf16[256,512]{1,0:T(8,128)(2,1)S(1)} fusion(f32[256,512]{1,0:T(8,128)} %get-tuple-element.20, bf16[256,512]{1,0:T(8,128)(2,1)S(1)} %collective-permute-done.7), kind=kLoop, calls=%fused_computation.3 | loop fusion | flops 393216 | bytes 1048576 | tf_op jit(solution)/shard_map/convert_element_type | solution.py:242
  50.9 1.3 %collective-permute-start.8 = (bf16[256,512]{1,0:T(8,128)(2,1)S(1)}, bf16[256,512]{1,0:T(8,128)(2,1)S(1)}, u32[]{:S(2)}, u32[]{:S(2)}) collective-permute-start(bf16[256,512]{1,0:T(8,128)(2,1)S(1)} %add_convert_fusion.1), channel_id=1, source_target_pairs={{4,0},{5,1},{6,2},{7,3},{12,8},{13,9},{14,10},{15,11},{20,16},{21,... | collective-permute-start | bytes 786440 | tf_op jit(solution)/shard_map/ppermute | solution.py:232
  52.2 7.2 %collective-permute-done.6 = bf16[256,512]{1,0:T(8,128)(2,1)S(1)} collective-permute-done((bf16[256,512]{1,0:T(8,128)(2,1)}, bf16[256,512]{1,0:T(8,128)(2,1)S(1)}, u32[]{:S(2)}, u32[]{:S(2)}) %collective-permute-start.6) | collective-permute-done | bytes 262176 | tf_op jit(solution)/shard_map/ppermute | solution.py:232
  59.4 12.1 %collective-permute-done.8 = bf16[256,512]{1,0:T(8,128)(2,1)S(1)} collective-permute-done((bf16[256,512]{1,0:T(8,128)(2,1)S(1)}, bf16[256,512]{1,0:T(8,128)(2,1)S(1)}, u32[]{:S(2)}, u32[]{:S(2)}) %collective-permute-start.8) | collective-permute-done | bytes 262176 | tf_op jit(solution)/shard_map/ppermute | solution.py:232
  71.7 2.6 %collective-permute-start.11 = (bf16[128,512]{1,0:T(8,128)(2,1)S(1)}, bf16[128,512]{1,0:T(8,128)(2,1)S(1)}, u32[]{:S(2)}, u32[]{:S(2)}) collective-permute-start(bf16[128,512]{1,0:T(8,128)(2,1)S(1)} %get-tuple-element.31), channel_id=1, source_target_pairs={{0,24},{1,25},{2,26},{3,27},{4,28},{5,29},{6,30},{7,31},{8,0},{9,1... | collective-permute-start | bytes 393224 | tf_op jit(solution)/shard_map/ppermute | solution.py:182
  74.3 0.2 collective-permute-start.12
  74.4 1.2 %maximum_select_fusion = bf16[1,128,4096]{2,1,0:T(8,128)(2,1)} fusion(bf16[1,128,2048]{2,1,0:T(8,128)(2,1)S(1)} %bitcast.48, bf16[1,128,2048]{2,1,0:T(8,128)(2,1)S(1)} %bitcast.49, pred[]{:T(512)S(6)} %eq.20), kind=kLoop, calls=%fused_computation.1 | loop fusion | flops 4718592 | bytes 2097153 | tf_op jit(solution)/shard_map/jit(_where)/select_n | solution.py:251
  75.6 2.7 %collective-permute-done.11 = bf16[128,512]{1,0:T(8,128)(2,1)S(1)} collective-permute-done((bf16[128,512]{1,0:T(8,128)(2,1)S(1)}, bf16[128,512]{1,0:T(8,128)(2,1)S(1)}, u32[]{:S(2)}, u32[]{:S(2)}) %collective-permute-start.11) | collective-permute-done | bytes 131104 | tf_op jit(solution)/shard_map/ppermute | solution.py:182
  78.3 1.2 %collective-permute-done.12 = bf16[128,512]{1,0:T(8,128)(2,1)S(1)} collective-permute-done((bf16[128,512]{1,0:T(8,128)(2,1)S(1)}, bf16[128,512]{1,0:T(8,128)(2,1)S(1)}, u32[]{:S(2)}, u32[]{:S(2)}) %collective-permute-start.12) | collective-permute-done | bytes 131104 | tf_op jit(solution)/shard_map/ppermute | solution.py:182
  79.6 0.7 maximum_select_fusion.2
  80.3 0.7 maximum_select_fusion.1
  (27 shorter events, 0.5 us)
Async XLA Ops:
  1.6 6.2 %collective-permute-start = (bf16[128,512]{1,0:T(8,128)(2,1)S(1)}, bf16[128,512]{1,0:T(8,128)(2,1)S(1)}, u32[]{:S(2)}, u32[]{:S(2)}) collective-permute-start(bf16[128,512]{1,0:T(8,128)(2,1)S(1)} %pad_maximum_fusion.2), channel_id=1, source_target_pairs={{0,1},{1,0},{2,3},{3,2},{4,5},{5,4},{6,7},{7,6},{8,9},{9,8},{10,11... | collective-permute-start | bytes 393224 | tf_op jit(solution)/shard_map/ppermute | solution.py:196
  5.1 2.7 %collective-permute-start.1 = (s32[1,133]{1,0:T(1,128)S(1)}, s32[1,133]{1,0:T(1,128)S(1)}, u32[]{:S(2)}, u32[]{:S(2)}) collective-permute-start(s32[1,133]{1,0:T(1,128)S(1)} %bitcast.52), channel_id=1, source_target_pairs={{0,1},{1,0},{2,3},{3,2},{4,5},{5,4},{6,7},{7,6},{8,9},{9,8},{10,11... | collective-permute-start | bytes 1604 | tf_op jit(solution)/shard_map/ppermute | solution.py:195
  7.8 22.8 %collective-permute-start.2 = (bf16[128,4096]{1,0:T(8,128)(2,1)S(1)}, bf16[128,4096]{1,0:T(8,128)(2,1)S(1)}, u32[]{:S(2)}, u32[]{:S(2)}) collective-permute-start(bf16[128,4096]{1,0:T(8,128)(2,1)S(1)} %pad_maximum_fusion), channel_id=1, source_target_pairs={{0,1},{1,0},{2,3},{3,2},{4,5},{5,4},{6,7},{7,6},{8,9},{9,8},{10,11... | collective-permute-start | bytes 3145736 | tf_op jit(solution)/shard_map/ppermute | solution.py:201
  8.2 22.4 %copy-start.1 = (bf16[256,512]{1,0:T(8,128)(2,1)}, bf16[256,512]{1,0:T(8,128)(2,1)S(1)}, u32[]{:S(2)}) copy-start(bf16[256,512]{1,0:T(8,128)(2,1)S(1)} %pad_maximum_fusion.1.refs_7_) | copy-start | bytes 786436
  8.2 10.9 %collective-permute-start.3 = (bf16[256,512]{1,0:T(8,128)(2,1)S(1)}, bf16[256,512]{1,0:T(8,128)(2,1)S(1)}, u32[]{:S(2)}, u32[]{:S(2)}) collective-permute-start(bf16[256,512]{1,0:T(8,128)(2,1)S(1)} %pad_maximum_fusion.1.refs_7_), channel_id=1, source_target_pairs={{0,2},{1,3},{2,4},{3,5},{4,6},{5,7},{8,10},{9,11},{10,12},{11,13},... | collective-permute-start | bytes 786440 | tf_op jit(solution)/shard_map/ppermute | solution.py:205
  11.5 10.3 %collective-permute-start.4 = (bf16[256,512]{1,0:T(8,128)(2,1)S(1)}, bf16[256,512]{1,0:T(8,128)(2,1)S(1)}, u32[]{:S(2)}, u32[]{:S(2)}) collective-permute-start(bf16[256,512]{1,0:T(8,128)(2,1)S(1)} %pad_maximum_fusion.1.refs_7_), channel_id=1, source_target_pairs={{0,4},{1,5},{2,6},{3,7},{8,12},{9,13},{10,14},{11,15},{16,20},{17,... | collective-permute-start | bytes 786440 | tf_op jit(solution)/shard_map/ppermute | solution.py:205
  15.7 11.7 %collective-permute-start.5 = (bf16[256,512]{1,0:T(8,128)(2,1)S(1)}, bf16[256,512]{1,0:T(8,128)(2,1)S(1)}, u32[]{:S(2)}, u32[]{:S(2)}) collective-permute-start(bf16[256,512]{1,0:T(8,128)(2,1)S(1)} %pad_maximum_fusion.1.refs_7_), channel_id=1, source_target_pairs={{0,6},{1,7},{8,14},{9,15},{16,22},{17,23},{24,30},{25,31}} | collective-permute-start | bytes 786440 | tf_op jit(solution)/shard_map/ppermute | solution.py:205
  19.1 11.5 %copy-start.3 = (bf16[256,512]{1,0:T(8,128)(2,1)}, bf16[256,512]{1,0:T(8,128)(2,1)S(1)}, u32[]{:S(2)}) copy-start(bf16[256,512]{1,0:T(8,128)(2,1)S(1)} %collective-permute-done.3.refs_8_) | copy-start | bytes 786436
  21.8 8.8 %copy-start.4 = (bf16[256,512]{1,0:T(8,128)(2,1)}, bf16[256,512]{1,0:T(8,128)(2,1)S(1)}, u32[]{:S(2)}) copy-start(bf16[256,512]{1,0:T(8,128)(2,1)S(1)} %collective-permute-done.4.refs_9_) | copy-start | bytes 786436
  27.4 3.2 %copy-start.5 = (bf16[256,512]{1,0:T(8,128)(2,1)}, bf16[256,512]{1,0:T(8,128)(2,1)S(1)}, u32[]{:S(2)}) copy-start(bf16[256,512]{1,0:T(8,128)(2,1)S(1)} %collective-permute-done.5.refs_10_) | copy-start | bytes 786436
  30.6 1.0 %copy-start.2 = (bf16[128,4096]{1,0:T(8,128)(2,1)}, bf16[128,4096]{1,0:T(8,128)(2,1)S(1)}, u32[]{:S(2)}) copy-start(bf16[128,4096]{1,0:T(8,128)(2,1)S(1)} %collective-permute-done.2.refs_6_) | copy-start | bytes 3145732
  44.6 27.0 %copy-start = (f32[256,512]{1,0:T(8,128)S(1)}, f32[256,512]{1,0:T(8,128)}, u32[]{:S(2)}) copy-start(f32[256,512]{1,0:T(8,128)} %get-tuple-element.26) | copy-start | bytes 1572868
  44.6 5.2 %collective-permute-start.7 = (bf16[256,512]{1,0:T(8,128)(2,1)}, bf16[256,512]{1,0:T(8,128)(2,1)S(1)}, u32[]{:S(2)}, u32[]{:S(2)}) collective-permute-start(bf16[256,512]{1,0:T(8,128)(2,1)} %get-tuple-element.21), channel_id=1, source_target_pairs={{6,4},{7,5},{14,12},{15,13},{22,20},{23,21},{30,28},{31,29}} | collective-permute-start | bytes 786440 | tf_op jit(solution)/shard_map/ppermute | solution.py:241
  45.4 26.1 %collective-permute-start.10 = (bf16[128,2048]{1,0:T(8,128)(2,1)}, bf16[128,2048]{1,0:T(8,128)(2,1)S(1)}, u32[]{:S(2)}, u32[]{:S(2)}) collective-permute-start(bf16[128,2048]{1,0:T(8,128)(2,1)} %get-tuple-element.23), channel_id=1, source_target_pairs={{0,25},{1,24},{2,27},{3,26},{4,29},{5,28},{6,31},{7,30},{8,1},{9,0... | collective-permute-start | bytes 1572872 | tf_op jit(solution)/shard_map/ppermute | solution.py:182
  48.5 23.1 %collective-permute-start.9 = (bf16[128,2048]{1,0:T(8,128)(2,1)}, bf16[128,2048]{1,0:T(8,128)(2,1)S(1)}, u32[]{:S(2)}, u32[]{:S(2)}) collective-permute-start(bf16[128,2048]{1,0:T(8,128)(2,1)} %get-tuple-element.22), channel_id=1, source_target_pairs={{0,24},{1,25},{2,26},{3,27},{4,28},{5,29},{6,30},{7,31},{8,0},{9,1... | collective-permute-start | bytes 1572872 | tf_op jit(solution)/shard_map/ppermute | solution.py:182
  48.5 10.9 %collective-permute-start.6 = (bf16[256,512]{1,0:T(8,128)(2,1)}, bf16[256,512]{1,0:T(8,128)(2,1)S(1)}, u32[]{:S(2)}, u32[]{:S(2)}) collective-permute-start(bf16[256,512]{1,0:T(8,128)(2,1)} %get-tuple-element.19), channel_id=1, source_target_pairs={{2,0},{3,1},{4,2},{5,3},{6,4},{7,5},{10,8},{11,9},{12,10},{13,11},... | collective-permute-start | bytes 786440 | tf_op jit(solution)/shard_map/ppermute | solution.py:232
  50.9 20.6 %collective-permute-start.8 = (bf16[256,512]{1,0:T(8,128)(2,1)S(1)}, bf16[256,512]{1,0:T(8,128)(2,1)S(1)}, u32[]{:S(2)}, u32[]{:S(2)}) collective-permute-start(bf16[256,512]{1,0:T(8,128)(2,1)S(1)} %add_convert_fusion.1), channel_id=1, source_target_pairs={{4,0},{5,1},{6,2},{7,3},{12,8},{13,9},{14,10},{15,11},{20,16},{21,... | collective-permute-start | bytes 786440 | tf_op jit(solution)/shard_map/ppermute | solution.py:232
  71.7 6.6 %collective-permute-start.11 = (bf16[128,512]{1,0:T(8,128)(2,1)S(1)}, bf16[128,512]{1,0:T(8,128)(2,1)S(1)}, u32[]{:S(2)}, u32[]{:S(2)}) collective-permute-start(bf16[128,512]{1,0:T(8,128)(2,1)S(1)} %get-tuple-element.31), channel_id=1, source_target_pairs={{0,24},{1,25},{2,26},{3,27},{4,28},{5,29},{6,30},{7,31},{8,0},{9,1... | collective-permute-start | bytes 393224 | tf_op jit(solution)/shard_map/ppermute | solution.py:182
  74.3 5.3 %collective-permute-start.12 = (bf16[128,512]{1,0:T(8,128)(2,1)S(1)}, bf16[128,512]{1,0:T(8,128)(2,1)S(1)}, u32[]{:S(2)}, u32[]{:S(2)}) collective-permute-start(bf16[128,512]{1,0:T(8,128)(2,1)S(1)} %get-tuple-element.32), channel_id=1, source_target_pairs={{0,25},{1,24},{2,27},{3,26},{4,29},{5,28},{6,31},{7,30},{8,1},{9,0... | collective-permute-start | bytes 393224 | tf_op jit(solution)/shard_map/ppermute | solution.py:182

commit v2 on v1

v2 whole, which is shorter than its diff:
```python
import math

import jax
import jax.numpy as jnp
from jax import lax
from jax.experimental import pallas as pl
from jax.experimental.pallas import tpu as pltpu
from jax.sharding import PartitionSpec as P

QUERY_HEADS = 32
KEY_VALUE_HEADS = 4
HEAD_SIZE = 128
BLOCK = 128
LIST = 4
GROUP = QUERY_HEADS // KEY_VALUE_HEADS
HALF_KV = KEY_VALUE_HEADS // 2
HALF_Q = QUERY_HEADS // 2 * HEAD_SIZE
KV_COLS = HALF_KV * HEAD_SIZE
WIDE = GROUP * HEAD_SIZE
PAIR = 2 * HEAD_SIZE
MASKED = -1e30
NONE, WHOLE, CAUSAL = 0, 1, 2

SCALE = 1.0 / math.sqrt(HEAD_SIZE)
FACTOR = SCALE / math.log(2.0)


def dot(a, b, contract):
    return lax.dot_general(
        a, b, ((contract[0], contract[1]), ((), ())), preferred_element_type=jnp.float32
    )


def attention_kernel(levels, *refs):
    place_ref, mode_ref, side_ref, segs_ref = refs[:4]
    query_ref, grad_ref, partner_ref = refs[4:7]
    held = refs[7 : 7 + levels][::-1]
    outs = refs[7 + levels : 9 + levels]
    term_refs = refs[9 + levels : 9 + 2 * levels]
    scratch = refs[9 + 2 * levels :]
    rows_of = [pl.ds(2 * j * BLOCK, 2 * BLOCK) for j in range(levels - 1)]
    rows_of.append(pl.ds(pl.multiple_of(2 * side_ref[1] * BLOCK, 2 * BLOCK), 2 * BLOCK))
    kv, rows_in, rows_out, bias, probs, dscores, sums = scratch[:7]
    terms = scratch[7 : 7 + levels]
    arrived, left = scratch[-2:]

    first_col = side_ref[0] * HALF_Q
    arrivals = []
    for group in range(HALF_KV):
        at = pl.ds(group * PAIR, PAIR)
        copies = [
            pltpu.make_async_copy(
                held[j].at[:, at],
                kv.at[pl.ds(2 * j * BLOCK, 2 * BLOCK), at],
                arrived.at[group, j],
            )
            for j in range(levels)
        ]
        blocks = []
        for block in range(2):
            pair = []
            for which, ref in enumerate((query_ref, grad_ref)):
                if block == 0:
                    start = pl.multiple_of(first_col + group * WIDE, WIDE)
                    source = ref.at[:, pl.ds(start, WIDE)]
                else:
                    source = partner_ref.at[:, pl.ds(which * HALF_Q + group * WIDE, WIDE)]
                pair.append(
                    pltpu.make_async_copy(
                        source,
                        rows_in.at[block, which, :, pl.ds(group * WIDE, WIDE)],
                        arrived.at[group, levels + 2 * block + which],
                    )
                )
            blocks.append(pair)
        arrivals.append((copies, blocks))
    for copies, blocks in arrivals:
        for copy in copies + blocks[0] + blocks[1]:
            copy.start()
    sums[...] = jnp.zeros_like(sums)

    key_at = lax.broadcasted_iota(jnp.int32, (BLOCK, BLOCK), 0)
    query_at = lax.broadcasted_iota(jnp.int32, (BLOCK, BLOCK), 1)
    shifts = []
    places = []
    for block in range(2):
        seg_of_query = jnp.broadcast_to(segs_ref[block : block + 1, :], (BLOCK, BLOCK))
        causal = (key_at <= query_at) & (seg_of_query.T == seg_of_query)
        mode = mode_ref[block * LIST]
        bias[block] = jnp.where((mode == CAUSAL) & causal, 0.0, MASKED)
        shifts.append(
            [
                jnp.where(mode_ref[block * LIST + slot] == WHOLE, 0.0, -MASKED)
                for slot in range(1, LIST)
            ]
        )
        places.append(
            [
                pl.ds(pl.multiple_of(place_ref[block * LIST + slot] * BLOCK, BLOCK), BLOCK)
                for slot in range(LIST)
            ]
        )

    departures = []

    def send(source, target):
        copy = pltpu.make_async_copy(source, target, left.at[len(departures)])
        copy.start()
        departures.append(copy)

    for group in range(HALF_KV):
        copies, blocks = arrivals[group]
        for copy in copies:
            copy.wait()
        key_cols = slice(group * PAIR, group * PAIR + HEAD_SIZE)
        value_cols = slice(group * PAIR + HEAD_SIZE, (group + 1) * PAIR)
        heads = [group * GROUP + h for h in range(GROUP)]
        for block in range(2):
            for copy in blocks[block]:
                copy.wait()

            def rows(which, head):
                return rows_in[block, which, :, head * HEAD_SIZE : (head + 1) * HEAD_SIZE]

            keys = jnp.concatenate([kv[at, key_cols] for at in places[block]], axis=0)
            values = jnp.concatenate([kv[at, value_cols] for at in places[block]], axis=0)
            shift = shifts[block]

            def products(h):
                query = jnp.concatenate([rows(0, heads[h]), rows(0, heads[h + 1])], axis=0)
                grad = jnp.concatenate([rows(1, heads[h]), rows(1, heads[h + 1])], axis=0)
                each = [slice(slot * BLOCK, (slot + 1) * BLOCK) for slot in range(LIST)]
                return (
                    [dot(keys[at], query, ((1,), (1,))) for at in each],
                    [dot(values[at], grad, ((1,), (1,))) for at in each],
                )

            for h in range(0, GROUP, 2):
                scores, dprobs = products(h)
                parts = list(scores)
                parts[0] = parts[0] + jnp.concatenate([bias[block], bias[block]], axis=1)

                def fold(value, by):
                    return by(value.reshape(BLOCK // 8, 8, 2 * BLOCK), axis=0)

                peak = fold(parts[0], jnp.max)
                for slot in range(1, LIST):
                    peak = jnp.maximum(peak, fold(parts[slot], jnp.max) - shift[slot - 1])
                peak = jnp.max(peak, axis=0, keepdims=True) * FACTOR
                peaks = [peak] + [peak + shift[slot - 1] for slot in range(1, LIST)]
                total = jnp.zeros((8, 2 * BLOCK), jnp.float32)
                mixed = jnp.zeros((8, 2 * BLOCK), jnp.float32)
                weights = []
                for slot in range(LIST):
                    weight = jnp.exp2(parts[slot] * FACTOR - peaks[slot])
                    total = total + fold(weight, jnp.sum)
                    mixed = mixed + fold(weight * dprobs[slot], jnp.sum)
                    weights.append(weight)
                inverse = 1.0 / jnp.sum(total, axis=0, keepdims=True)
                delta = jnp.sum(mixed, axis=0, keepdims=True) * inverse
                at = slice(h * BLOCK, (h + 2) * BLOCK)
                for slot in range(LIST):
                    full = weights[slot] * inverse
                    down = slice(slot * BLOCK, (slot + 1) * BLOCK)
                    probs[down, at] = full.astype(jnp.bfloat16)
                    dscores[down, at] = (full * (dprobs[slot] - delta)).astype(jnp.bfloat16)
            query_all = jnp.concatenate([rows(0, head) for head in heads], axis=0)
            grad_all = jnp.concatenate([rows(1, head) for head in heads], axis=0)
            query_grad = dot(dscores[...], keys, ((0,), (0,))) * SCALE
            for h, head in enumerate(heads):
                rows_out[block, :, head * HEAD_SIZE : (head + 1) * HEAD_SIZE] = query_grad[
                    h * BLOCK : (h + 1) * BLOCK
                ].astype(jnp.bfloat16)
            wide = pl.ds(group * WIDE, WIDE)
            send(rows_out.at[block, :, wide], outs[block].at[:, wide])
            key_terms = dot(dscores[...], query_all, ((1,), (0,))) * SCALE
            value_terms = dot(probs[...], grad_all, ((1,), (0,)))
            for slot in range(LIST):
                at = slice(slot * BLOCK, (slot + 1) * BLOCK)
                sums[places[block][slot], key_cols] += key_terms[at]
                sums[places[block][slot], value_cols] += value_terms[at]
        cols = slice(group * PAIR, (group + 1) * PAIR)
        for j in range(levels):
            terms[j][:, cols] = sums[rows_of[j], cols].astype(terms[j].dtype)
            cut = pl.ds(group * PAIR, PAIR)
            send(terms[j].at[:, cut], term_refs[j].at[:, cut])
    for copy in departures:
        copy.wait()


def attention(levels, place, mode, side, segs, queries, grads, partner, held):
    smem = pl.BlockSpec(memory_space=pltpu.SMEM)
    anywhere = pl.BlockSpec(memory_space=pl.ANY)
    keys = LIST * BLOCK
    width = HALF_KV * PAIR
    outs = [jax.ShapeDtypeStruct((BLOCK, HALF_Q), jnp.bfloat16)] * 2
    terms = [
        jax.ShapeDtypeStruct(
            (2 * BLOCK, width), jnp.bfloat16 if j in (1, levels - 1) else jnp.float32
        )
        for j in range(levels)
    ]
    return pl.pallas_call(
        lambda *refs: attention_kernel(levels, *refs),
        out_shape=outs + terms,
        in_specs=[smem, smem, smem, pl.BlockSpec(memory_space=pltpu.VMEM)]
        + [anywhere] * (3 + levels),
        out_specs=[anywhere] * (2 + levels),
        scratch_shapes=[
            pltpu.VMEM((2 * levels * BLOCK, width), jnp.bfloat16),
            pltpu.VMEM((2, 2, BLOCK, HALF_Q), jnp.bfloat16),
            pltpu.VMEM((2, BLOCK, HALF_Q), jnp.bfloat16),
            pltpu.VMEM((2, BLOCK, BLOCK), jnp.float32),
            pltpu.VMEM((keys, WIDE), jnp.bfloat16),
            pltpu.VMEM((keys, WIDE), jnp.bfloat16),
            pltpu.VMEM((2 * levels * BLOCK, width), jnp.float32),
        ]
        + [pltpu.VMEM(term.shape, term.dtype) for term in terms]
        + [
            pltpu.SemaphoreType.DMA((HALF_KV, levels + 4)),
            pltpu.SemaphoreType.DMA((HALF_KV * (levels + 2),)),
        ],
        compiler_params=pltpu.CompilerParams(vmem_limit_bytes=60 * 1024 * 1024),
        cost_estimate=pl.CostEstimate(
            flops=5 * 2 * keys * HEAD_SIZE * BLOCK * QUERY_HEADS,
            bytes_accessed=8 * 1024 * 1024,
            transcendentals=keys * BLOCK * QUERY_HEADS,
        ),
    )(place, mode, side, segs, queries, grads, partner, *held[::-1])


def per_device(
    queries, key_heads, value_per_head, out_grads, segment_ids, block_lists, list_counts
):
    sections = lax.axis_size("section")
    blocks = lax.axis_size("blk")
    levels = blocks // 2
    mine = lax.axis_index("blk")
    side = mine % 2
    level = mine // 2
    swap = [(i, i ^ 1) for i in range(blocks)]

    def back(value, moved):
        pairs = [
            (s * blocks + b, (s - 1) % sections * blocks + moved(b))
            for s in range(sections)
            for b in range(blocks)
            if moved(b) >= 0
        ]
        return lax.ppermute(value, ("section", "blk"), pairs)

    def columns(array, start, width):
        return lax.dynamic_slice_in_dim(array[0], start, width, 1)

    def heads_of(half):
        parts = []
        for g in range(HALF_KV):
            start = half * KV_COLS + g * HEAD_SIZE
            parts += [columns(a, start, HEAD_SIZE) for a in (key_heads, value_per_head)]
        return jnp.concatenate(parts, axis=1)

    facts = jnp.concatenate([segment_ids[0], block_lists[0, 0], list_counts[0]])[None]
    facts_got = lax.ppermute(facts, "blk", swap)
    other = lax.ppermute(heads_of(1 - side), "blk", swap)
    theirs = jnp.concatenate(
        [columns(a, (1 - side) * HALF_Q, HALF_Q) for a in (queries, out_grads)], axis=1
    )
    theirs, other, facts_got = lax.optimization_barrier((theirs, other, facts_got))
    partner = lax.ppermute(theirs, "blk", swap)
    held = [jnp.concatenate([heads_of(side), other], axis=0)]
    for hop in range(1, levels):
        pairs = [(i, i + 2 * hop) for i in range(blocks - 2 * hop)]
        held.append(lax.ppermute(held[0], "blk", pairs))

    facts = jnp.concatenate([facts, facts_got], axis=0)
    segs = facts[:, :BLOCK]
    lists = facts[:, BLOCK : BLOCK + LIST]
    counts = facts[:, BLOCK + LIST :]
    block = jnp.stack([mine, mine ^ 1])[:, None].astype(jnp.int32)
    listed = jnp.arange(LIST, dtype=jnp.int32)[None, :] < counts
    mode = jnp.where(lists == block, CAUSAL, jnp.where(lists < block, WHOLE, NONE))
    mode = jnp.where(listed, mode, NONE).astype(jnp.int32)
    place = 2 * (level - lists // 2) + (lists % 2 != side).astype(jnp.int32)
    place = jnp.where(mode == NONE, 0, place).astype(jnp.int32)

    top = levels - 1
    own_out, partner_out, here, near, *between, first = attention(
        levels,
        place.reshape(-1),
        mode.reshape(-1),
        jnp.stack([side, jnp.where(level == top, top, 1)]).astype(jnp.int32),
        segs,
        queries[0],
        out_grads[0],
        partner,
        held,
    )

    def down(terms, hop, lowest):
        pairs = [(i, i - 2 * hop) for i in range(2 * lowest, blocks)]
        return lax.ppermute(terms, "blk", pairs)

    landed = down(first, 1, 1)
    query_grads = (back(own_out, lambda b: b), back(partner_out, lambda b: b ^ 1))
    carried = landed
    for j in range(top - 1, 1, -1):
        total = between[j - 2] + carried.astype(jnp.float32)
        total = total.astype(jnp.bfloat16)
        carried = down(total, 1, j) if j > 2 else down(total, 2, 2)
    here = here + jnp.where(level == top - 1, 0.0, landed.astype(jnp.float32))
    near, here = lax.optimization_barrier((near, here))
    rest = down(near, 1, top)
    rest, query_grads, carried = lax.optimization_barrier((rest, query_grads, carried))
    totals = (here + carried.astype(jnp.float32) + rest.astype(jnp.float32)).astype(jnp.bfloat16)
    sums = [back(totals[:BLOCK], lambda b: b), back(totals[BLOCK:], lambda b: b ^ 1)]

    def ordered(a, b):
        return jnp.where(side == 0, jnp.concatenate([a, b], axis=1), jnp.concatenate([b, a], axis=1))

    grad_queries = ordered(*query_grads)

    def kind(total, which):
        starts = [g * PAIR + which * HEAD_SIZE for g in range(HALF_KV)]
        return jnp.concatenate([total[:, at : at + HEAD_SIZE] for at in starts], axis=1)

    grad_keys = ordered(kind(sums[0], 0), kind(sums[1], 0))
    grad_values = ordered(kind(sums[0], 1), kind(sums[1], 1))
    return (grad_queries[None], grad_keys[None], grad_values[None])


def solution(mesh):
    in_specs = (
        P("section", "blk", None),
        P("section", "blk", None),
        P("section", "blk", None),
        P("section", "blk", None),
        P("section", "blk"),
        P("section", "blk", None),
        P("section", "blk"),
    )
    out_specs = (P("section", "blk", None), P("section", "blk", None), P("section", "blk", None))
    return jax.shard_map(
        per_device, mesh=mesh, in_specs=in_specs, out_specs=out_specs, check_vma=False
    )
```

time: 81.4 us -> 78.6 us (0.966); the launches traced: 80.9 us -> 77.2 us
  waiting for transfers between devices: 36 us -> 27.9 us
  starting transfers between devices: 20.4 us -> 25.6 us
  Pallas kernels: 13 us -> 11.4 us
  other arithmetic: 5.58 us -> 6.44 us
    ppermute x3, waiting for transfers between devices: 19.3 us -> 11.1 us  [down(): return lax.ppermute(terms, 'blk', pairs)]
    ppermute x4, starting transfers between devices: 5.79 us -> 11.2 us  [back(): return lax.ppermute(value, ('section', 'blk'), pairs)]
    ppermute x1, waiting for transfers between devices: 0.01 us -> 2.4 us  [per_device(): other = lax.ppermute(heads_of(1 - side), 'blk', swap)]
    ppermute x1, starting transfers between devices: 2.13 us -> 0.07 us  [per_device(): other = lax.ppermute(heads_of(1 - side), 'blk', swap)]
    ppermute x1, starting transfers between devices: 0.01 us -> 2.07 us  [per_device(): facts_got = lax.ppermute(facts, 'blk', swap)]
    pallas_call x1, Pallas kernels: 13 us -> 11.4 us  [attention(): pl.pallas_call(lambda *refs: attention_kernel(levels, *refs), out_shape=o...]
    ppermute x1, waiting for transfers between devices: 1.26 us -> 0.01 us  [per_device(): facts_got = lax.ppermute(facts, 'blk', swap)]
  transfers between devices with their start and end apart: 13 -> 13, of which waited for: 8 -> 8; matrix products, arithmetic and copies ran while one was open for 8% -> 10% of each run, Pallas kernels for 0% -> 0%
where the time goes in v2:
time: 78.6 us; the launch traced here: 77.2 us
  waiting for transfers between devices  27.9 us (35%)
  starting transfers between devices  25.6 us (33%)
  Pallas kernels  11.4 us (15%)
  other arithmetic  6.44 us (8%)
  local copies, waits for them, and re-layouts  4.45 us (6%)
  between operations  1.48 us (2%)
    pallas_call x1, Pallas kernels, attention(): pl.pallas_call(lambda *refs: attention_kernel(levels, *refs), out_shape=o...  11.4 us
    ppermute x4, starting transfers between devices, back(): return lax.ppermute(value, ('section', 'blk'), pairs)  11.2 us
    ppermute x3, waiting for transfers between devices, down(): return lax.ppermute(terms, 'blk', pairs)  11.1 us
    ppermute x3, starting transfers between devices, per_device(): held.append(lax.ppermute(held[0], 'blk', pairs))  8.39 us
    ppermute x3, waiting for transfers between devices, per_device(): held.append(lax.ppermute(held[0], 'blk', pairs))  8.04 us
    ppermute x4, waiting for transfers between devices, back(): return lax.ppermute(value, ('section', 'blk'), pairs)  3.7 us
    ppermute x3, starting transfers between devices, down(): return lax.ppermute(terms, 'blk', pairs)  3.26 us
    ppermute x1, waiting for transfers between devices, per_device(): partner = lax.ppermute(theirs, 'blk', swap)  2.73 us
  transfers between devices with their start and end apart: 13, of which 8 were waited for; matrix products, arithmetic and copies ran while one was open for 10% of the time, Pallas kernels for 0%

profile of v2, /device:TPU:1, one launch (start us, length us, event | category | flops | bytes accessed | tf_op | source)
XLA Modules:
  0.0 77.2 jit_solution(2857279135356906830)
XLA Ops:
  1.3 0.7 pad_add_fusion.1
  2.0 2.1 %collective-permute-start.1 = (s32[1,133]{1,0:T(1,128)S(1)}, s32[1,133]{1,0:T(1,128)S(1)}, u32[]{:S(2)}, u32[]{:S(2)}) collective-permute-start(s32[1,133]{1,0:T(1,128)S(1)} %bitcast.53), channel_id=1, source_target_pairs={{0,1},{1,0},{2,3},{3,2},{4,5},{5,4},{6,7},{7,6},{8,9},{9,8},{10,11... | collective-permute-start | bytes 1604 | tf_op jit(solution)/shard_map/ppermute | solution.py:263
  4.1 0.9 %dynamic-slice_bitcast_fusion.4 = (bf16[128,128]{1,0:T(8,128)(2,1)S(1)}, bf16[128,128]{1,0:T(8,128)(2,1)S(1)}, bf16[128,128]{1,0:T(8,128)(2,1)S(1)}, bf16[128,12...) fusion(bf16[1,128,512]{2,1,0:T(8,128)(2,1)} %param.9, ...), kind=kLoop, calls=%fused_computation.23 | loop fusion | bytes 524304 | tf_op jit(solution)/shard_map/dynamic_slice | solution.py:253
  5.1 1.3 %dynamic-slice_bitcast_fusion = (bf16[128,2048]{1,0:T(8,128)(2,1)S(1)}, bf16[128,2048]{1,0:T(8,128)(2,1)S(1)}) fusion(bf16[1,128,4096]{2,1,0:T(8,128)(2,1)} %param.10, s32[]{:T(128)S(6)} %select_n.113, bf16[1,128,4096]{2,1,0:T(8,128)(2,1)} %param.7), kind=kLoop, calls=%fused_computation.7 | loop fusion | bytes 2097156 | tf_op jit(solution)/shard_map/dynamic_slice | solution.py:253
  6.5 2.4 %collective-permute-done = bf16[128,512]{1,0:T(8,128)(2,1)S(1)} collective-permute-done((bf16[128,512]{1,0:T(8,128)(2,1)S(1)}, bf16[128,512]{1,0:T(8,128)(2,1)S(1)}, u32[]{:S(2)}, u32[]{:S(2)}) %collective-permute-start) | collective-permute-done | bytes 131104 | tf_op jit(solution)/shard_map/ppermute | solution.py:264
  8.9 0.6 collective-permute-start.2
  9.5 0.6 pad_add_fusion.3.refs_2_
  10.2 2.9 %collective-permute-start.5 = (bf16[256,512]{1,0:T(8,128)(2,1)S(1)}, bf16[256,512]{1,0:T(8,128)(2,1)S(1)}, u32[]{:S(2)}, u32[]{:S(2)}) collective-permute-start(bf16[256,512]{1,0:T(8,128)(2,1)S(1)} %pad_maximum_fusion.1.refs_10_), channel_id=1, source_target_pairs={{0,2},{1,3},{2,4},{3,5},{4,6},{5,7},{8,10},{9,11},{10,12},{11,13},... | collective-permute-start | bytes 786440 | tf_op jit(solution)/shard_map/ppermute | solution.py:273
  13.1 4.2 %collective-permute-start.4 = (bf16[256,512]{1,0:T(8,128)(2,1)S(1)}, bf16[256,512]{1,0:T(8,128)(2,1)S(1)}, u32[]{:S(2)}, u32[]{:S(2)}) collective-permute-start(bf16[256,512]{1,0:T(8,128)(2,1)S(1)} %pad_maximum_fusion.1.refs_10_), channel_id=1, source_target_pairs={{0,4},{1,5},{2,6},{3,7},{8,12},{9,13},{10,14},{11,15},{16,20},{17,... | collective-permute-start | bytes 786440 | tf_op jit(solution)/shard_map/ppermute | solution.py:273
  17.3 1.3 %collective-permute-start.3 = (bf16[256,512]{1,0:T(8,128)(2,1)S(1)}, bf16[256,512]{1,0:T(8,128)(2,1)S(1)}, u32[]{:S(2)}, u32[]{:S(2)}) collective-permute-start(bf16[256,512]{1,0:T(8,128)(2,1)S(1)} %pad_maximum_fusion.1.refs_10_), channel_id=1, source_target_pairs={{0,6},{1,7},{8,14},{9,15},{16,22},{17,23},{24,30},{25,31}} | collective-permute-start | bytes 786440 | tf_op jit(solution)/shard_map/ppermute | solution.py:273
  18.9 0.6 reshape.292.refs_0_
  19.4 0.7 reshape.293.refs_1_
  20.1 0.6 pad_add_fusion.refs_3_
  20.7 2.4 %collective-permute-done.4.refs_8_ = bf16[256,512]{1,0:T(8,128)(2,1)S(1)} collective-permute-done((bf16[256,512]{1,0:T(8,128)(2,1)S(1)}, bf16[256,512]{1,0:T(8,128)(2,1)S(1)}, u32[]{:S(2)}, u32[]{:S(2)}) %collective-permute-start.4) | collective-permute-done | bytes 262176 | tf_op jit(solution)/shard_map/ppermute | solution.py:273
  23.1 5.6 %collective-permute-done.3.refs_7_ = bf16[256,512]{1,0:T(8,128)(2,1)S(1)} collective-permute-done((bf16[256,512]{1,0:T(8,128)(2,1)S(1)}, bf16[256,512]{1,0:T(8,128)(2,1)S(1)}, u32[]{:S(2)}, u32[]{:S(2)}) %collective-permute-start.3) | collective-permute-done | bytes 262176 | tf_op jit(solution)/shard_map/ppermute | solution.py:273
  28.7 2.7 %collective-permute-done.2.refs_6_ = bf16[128,4096]{1,0:T(8,128)(2,1)S(1)} collective-permute-done((bf16[128,4096]{1,0:T(8,128)(2,1)S(1)}, bf16[128,4096]{1,0:T(8,128)(2,1)S(1)}, u32[]{:S(2)}, u32[]{:S(2)}) %collective-permute-start.2) | collective-permute-done | bytes 1048608 | tf_op jit(solution)/shard_map/ppermute | solution.py:269
  31.5 0.9 %copy-done.1 = bf16[128,4096]{1,0:T(8,128)(2,1)} copy-done((bf16[128,4096]{1,0:T(8,128)(2,1)}, bf16[128,4096]{1,0:T(8,128)(2,1)S(1)}, u32[]{:S(2)}) %copy-start.1) | copy-done | bytes 1048600
  32.4 11.4 %shard_map.94 = (bf16[128,2048]{1,0:T(8,128)(2,1)}, bf16[128,2048]{1,0:T(8,128)(2,1)}, f32[256,512]{1,0:T(8,128)}, bf16[256,512]{1,0:T(8,128)(2,1)}, f32[256,512]{1,0:T(8,128)}, /*index=5*/bf16[256,512]{1,0:T(8,128)(2,1)}) custom-call(s32[8]{0:T(128)} %reshape.292.refs_0_, s32[8]{0:T(128)} %reshape.293.refs_1_, s32[2]{0:T(128)} %pad_add_fusion.3.refs_2_, ...), custom_call_target="tpu_custom_call" | custom-call | flops 2684354560 | bytes 8388608 | tf_op jit(solution)/shard_map/pallas_call | solution.py:203
  43.8 1.3 %collective-permute-start.6 = (bf16[256,512]{1,0:T(8,128)(2,1)}, bf16[256,512]{1,0:T(8,128)(2,1)S(1)}, u32[]{:S(2)}, u32[]{:S(2)}) collective-permute-start(bf16[256,512]{1,0:T(8,128)(2,1)} %get-tuple-element.23), channel_id=1, source_target_pairs={{2,0},{3,1},{4,2},{5,3},{6,4},{7,5},{10,8},{11,9},{12,10},{13,11},... | collective-permute-start | bytes 786440 | tf_op jit(solution)/shard_map/ppermute | solution.py:301
  45.1 3.1 %collective-permute-start.8 = (bf16[128,2048]{1,0:T(8,128)(2,1)}, bf16[128,2048]{1,0:T(8,128)(2,1)S(1)}, u32[]{:S(2)}, u32[]{:S(2)}) collective-permute-start(bf16[128,2048]{1,0:T(8,128)(2,1)} %get-tuple-element.25), channel_id=1, source_target_pairs={{0,24},{1,25},{2,26},{3,27},{4,28},{5,29},{6,30},{7,31},{8,0},{9,1... | collective-permute-start | bytes 1572872 | tf_op jit(solution)/shard_map/ppermute | solution.py:250
  48.7 4.4 %collective-permute-done.6 = bf16[256,512]{1,0:T(8,128)(2,1)S(1)} collective-permute-done((bf16[256,512]{1,0:T(8,128)(2,1)}, bf16[256,512]{1,0:T(8,128)(2,1)S(1)}, u32[]{:S(2)}, u32[]{:S(2)}) %collective-permute-start.6) | collective-permute-done | bytes 262176 | tf_op jit(solution)/shard_map/ppermute | solution.py:301
  53.1 1.4 %fusion.1 = (bf16[256,512]{1,0:T(8,128)(2,1)S(1)}, f32[256,512]{1,0:T(8,128)S(1)}) fusion(f32[256,512]{1,0:T(8,128)} %get-tuple-element.27, bf16[256,512]{1,0:T(8,128)(2,1)S(1)} %collective-permute-done.6, f32[256,512]{1,0:T(8,128)} %get-tuple-element.22, pred[]{:T(512)S(6)} %eq.31), kind=kLoop, calls=%fused_computation.5 | loop fusion | flops 655360 | bytes 2097153 | tf_op jit(solution)/shard_map/convert_element_type | solution.py:308
  54.5 0.7 collective-permute-start.7
  55.2 1.3 %collective-permute-start.10 = (bf16[256,512]{1,0:T(8,128)(2,1)S(1)}, bf16[256,512]{1,0:T(8,128)(2,1)S(1)}, u32[]{:S(2)}, u32[]{:S(2)}) collective-permute-start(bf16[256,512]{1,0:T(8,128)(2,1)S(1)} %get-tuple-element.37), channel_id=1, source_target_pairs={{4,0},{5,1},{6,2},{7,3},{12,8},{13,9},{14,10},{15,11},{20,16},{21,... | collective-permute-start | bytes 786440 | tf_op jit(solution)/shard_map/ppermute | solution.py:301
  56.5 6.7 %collective-permute-done.10 = bf16[256,512]{1,0:T(8,128)(2,1)S(1)} collective-permute-done((bf16[256,512]{1,0:T(8,128)(2,1)S(1)}, bf16[256,512]{1,0:T(8,128)(2,1)S(1)}, u32[]{:S(2)}, u32[]{:S(2)}) %collective-permute-start.10) | collective-permute-done | bytes 262176 | tf_op jit(solution)/shard_map/ppermute | solution.py:301
  63.3 6.4 %collective-permute-start.11 = (bf16[128,512]{1,0:T(8,128)(2,1)S(1)}, bf16[128,512]{1,0:T(8,128)(2,1)S(1)}, u32[]{:S(2)}, u32[]{:S(2)}) collective-permute-start(bf16[128,512]{1,0:T(8,128)(2,1)S(1)} %get-tuple-element.35), channel_id=1, source_target_pairs={{0,24},{1,25},{2,26},{3,27},{4,28},{5,29},{6,30},{7,31},{8,0},{9,1... | collective-permute-start | bytes 393224 | tf_op jit(solution)/shard_map/ppermute | solution.py:250
  69.7 1.2 %collective-permute-start.12 = (bf16[128,512]{1,0:T(8,128)(2,1)S(1)}, bf16[128,512]{1,0:T(8,128)(2,1)S(1)}, u32[]{:S(2)}, u32[]{:S(2)}) collective-permute-start(bf16[128,512]{1,0:T(8,128)(2,1)S(1)} %get-tuple-element.36), channel_id=1, source_target_pairs={{0,25},{1,24},{2,27},{3,26},{4,29},{5,28},{6,31},{7,30},{8,1},{9,0... | collective-permute-start | bytes 393224 | tf_op jit(solution)/shard_map/ppermute | solution.py:250
  70.9 1.2 %maximum_select_fusion = bf16[1,128,4096]{2,1,0:T(8,128)(2,1)} fusion(bf16[1,128,2048]{2,1,0:T(8,128)(2,1)S(1)} %bitcast.50, bf16[1,128,2048]{2,1,0:T(8,128)(2,1)S(1)} %bitcast.49, pred[]{:T(512)S(6)} %eq.26), kind=kLoop, calls=%fused_computation.1 | loop fusion | flops 4718592 | bytes 2097153 | tf_op jit(solution)/shard_map/jit(_where)/select_n | solution.py:318
  72.1 1.6 %collective-permute-done.11 = bf16[128,512]{1,0:T(8,128)(2,1)S(1)} collective-permute-done((bf16[128,512]{1,0:T(8,128)(2,1)S(1)}, bf16[128,512]{1,0:T(8,128)(2,1)S(1)}, u32[]{:S(2)}, u32[]{:S(2)}) %collective-permute-start.11) | collective-permute-done | bytes 131104 | tf_op jit(solution)/shard_map/ppermute | solution.py:250
  73.8 2.1 %collective-permute-done.12 = bf16[128,512]{1,0:T(8,128)(2,1)S(1)} collective-permute-done((bf16[128,512]{1,0:T(8,128)(2,1)S(1)}, bf16[128,512]{1,0:T(8,128)(2,1)S(1)}, u32[]{:S(2)}, u32[]{:S(2)}) %collective-permute-start.12) | collective-permute-done | bytes 131104 | tf_op jit(solution)/shard_map/ppermute | solution.py:250
  75.9 0.7 maximum_select_fusion.2
  76.6 0.7 maximum_select_fusion.1
  (28 shorter events, 1.3 us)
Async XLA Ops:
  2.0 4.5 %collective-permute-start.1 = (s32[1,133]{1,0:T(1,128)S(1)}, s32[1,133]{1,0:T(1,128)S(1)}, u32[]{:S(2)}, u32[]{:S(2)}) collective-permute-start(s32[1,133]{1,0:T(1,128)S(1)} %bitcast.53), channel_id=1, source_target_pairs={{0,1},{1,0},{2,3},{3,2},{4,5},{5,4},{6,7},{7,6},{8,9},{9,8},{10,11... | collective-permute-start | bytes 1604 | tf_op jit(solution)/shard_map/ppermute | solution.py:263
  5.0 3.9 %collective-permute-start = (bf16[128,512]{1,0:T(8,128)(2,1)S(1)}, bf16[128,512]{1,0:T(8,128)(2,1)S(1)}, u32[]{:S(2)}, u32[]{:S(2)}) collective-permute-start(bf16[128,512]{1,0:T(8,128)(2,1)S(1)} %pad_maximum_fusion.2), channel_id=1, source_target_pairs={{0,1},{1,0},{2,3},{3,2},{4,5},{5,4},{6,7},{7,6},{8,9},{9,8},{10,11... | collective-permute-start | bytes 393224 | tf_op jit(solution)/shard_map/ppermute | solution.py:264
  8.9 22.5 %collective-permute-start.2 = (bf16[128,4096]{1,0:T(8,128)(2,1)S(1)}, bf16[128,4096]{1,0:T(8,128)(2,1)S(1)}, u32[]{:S(2)}, u32[]{:S(2)}) collective-permute-start(bf16[128,4096]{1,0:T(8,128)(2,1)S(1)} %pad_maximum_fusion), channel_id=1, source_target_pairs={{0,1},{1,0},{2,3},{3,2},{4,5},{5,4},{6,7},{7,6},{8,9},{9,8},{10,11... | collective-permute-start | bytes 3145736 | tf_op jit(solution)/shard_map/ppermute | solution.py:269
  10.2 21.3 %copy-start = (bf16[256,512]{1,0:T(8,128)(2,1)}, bf16[256,512]{1,0:T(8,128)(2,1)S(1)}, u32[]{:S(2)}) copy-start(bf16[256,512]{1,0:T(8,128)(2,1)S(1)} %pad_maximum_fusion.1.refs_10_) | copy-start | bytes 786436
  10.2 10.5 %collective-permute-start.5 = (bf16[256,512]{1,0:T(8,128)(2,1)S(1)}, bf16[256,512]{1,0:T(8,128)(2,1)S(1)}, u32[]{:S(2)}, u32[]{:S(2)}) collective-permute-start(bf16[256,512]{1,0:T(8,128)(2,1)S(1)} %pad_maximum_fusion.1.refs_10_), channel_id=1, source_target_pairs={{0,2},{1,3},{2,4},{3,5},{4,6},{5,7},{8,10},{9,11},{10,12},{11,13},... | collective-permute-start | bytes 786440 | tf_op jit(solution)/shard_map/ppermute | solution.py:273
  13.1 10.0 %collective-permute-start.4 = (bf16[256,512]{1,0:T(8,128)(2,1)S(1)}, bf16[256,512]{1,0:T(8,128)(2,1)S(1)}, u32[]{:S(2)}, u32[]{:S(2)}) collective-permute-start(bf16[256,512]{1,0:T(8,128)(2,1)S(1)} %pad_maximum_fusion.1.refs_10_), channel_id=1, source_target_pairs={{0,4},{1,5},{2,6},{3,7},{8,12},{9,13},{10,14},{11,15},{16,20},{17,... | collective-permute-start | bytes 786440 | tf_op jit(solution)/shard_map/ppermute | solution.py:273
  17.3 11.4 %collective-permute-start.3 = (bf16[256,512]{1,0:T(8,128)(2,1)S(1)}, bf16[256,512]{1,0:T(8,128)(2,1)S(1)}, u32[]{:S(2)}, u32[]{:S(2)}) collective-permute-start(bf16[256,512]{1,0:T(8,128)(2,1)S(1)} %pad_maximum_fusion.1.refs_10_), channel_id=1, source_target_pairs={{0,6},{1,7},{8,14},{9,15},{16,22},{17,23},{24,30},{25,31}} | collective-permute-start | bytes 786440 | tf_op jit(solution)/shard_map/ppermute | solution.py:273
  20.7 10.8 %copy-start.3 = (bf16[256,512]{1,0:T(8,128)(2,1)}, bf16[256,512]{1,0:T(8,128)(2,1)S(1)}, u32[]{:S(2)}) copy-start(bf16[256,512]{1,0:T(8,128)(2,1)S(1)} %collective-permute-done.5.refs_9_) | copy-start | bytes 786436
  23.1 8.4 %copy-start.4 = (bf16[256,512]{1,0:T(8,128)(2,1)}, bf16[256,512]{1,0:T(8,128)(2,1)S(1)}, u32[]{:S(2)}) copy-start(bf16[256,512]{1,0:T(8,128)(2,1)S(1)} %collective-permute-done.4.refs_8_) | copy-start | bytes 786436
  28.7 2.7 %copy-start.5 = (bf16[256,512]{1,0:T(8,128)(2,1)}, bf16[256,512]{1,0:T(8,128)(2,1)S(1)}, u32[]{:S(2)}) copy-start(bf16[256,512]{1,0:T(8,128)(2,1)S(1)} %collective-permute-done.3.refs_7_) | copy-start | bytes 786436
  31.4 1.0 %copy-start.1 = (bf16[128,4096]{1,0:T(8,128)(2,1)}, bf16[128,4096]{1,0:T(8,128)(2,1)S(1)}, u32[]{:S(2)}) copy-start(bf16[128,4096]{1,0:T(8,128)(2,1)S(1)} %collective-permute-done.2.refs_6_) | copy-start | bytes 3145732
  43.8 9.3 %collective-permute-start.6 = (bf16[256,512]{1,0:T(8,128)(2,1)}, bf16[256,512]{1,0:T(8,128)(2,1)S(1)}, u32[]{:S(2)}, u32[]{:S(2)}) collective-permute-start(bf16[256,512]{1,0:T(8,128)(2,1)} %get-tuple-element.23), channel_id=1, source_target_pairs={{2,0},{3,1},{4,2},{5,3},{6,4},{7,5},{10,8},{11,9},{12,10},{13,11},... | collective-permute-start | bytes 786440 | tf_op jit(solution)/shard_map/ppermute | solution.py:301
  45.1 18.1 %collective-permute-start.8 = (bf16[128,2048]{1,0:T(8,128)(2,1)}, bf16[128,2048]{1,0:T(8,128)(2,1)S(1)}, u32[]{:S(2)}, u32[]{:S(2)}) collective-permute-start(bf16[128,2048]{1,0:T(8,128)(2,1)} %get-tuple-element.25), channel_id=1, source_target_pairs={{0,24},{1,25},{2,26},{3,27},{4,28},{5,29},{6,30},{7,31},{8,0},{9,1... | collective-permute-start | bytes 1572872 | tf_op jit(solution)/shard_map/ppermute | solution.py:250
  48.2 15.0 %collective-permute-start.9 = (bf16[128,2048]{1,0:T(8,128)(2,1)}, bf16[128,2048]{1,0:T(8,128)(2,1)S(1)}, u32[]{:S(2)}, u32[]{:S(2)}) collective-permute-start(bf16[128,2048]{1,0:T(8,128)(2,1)} %get-tuple-element.26), channel_id=1, source_target_pairs={{0,25},{1,24},{2,27},{3,26},{4,29},{5,28},{6,31},{7,30},{8,1},{9,0... | collective-permute-start | bytes 1572872 | tf_op jit(solution)/shard_map/ppermute | solution.py:250
  53.1 1.4 %copy-start.2 = (bf16[256,512]{1,0:T(8,128)(2,1)S(1)}, bf16[256,512]{1,0:T(8,128)(2,1)}, u32[]{:S(2)}) copy-start(bf16[256,512]{1,0:T(8,128)(2,1)} %get-tuple-element.24) | copy-start | bytes 786436
  54.5 2.0 %collective-permute-start.7 = (bf16[256,512]{1,0:T(8,128)(2,1)S(1)}, bf16[256,512]{1,0:T(8,128)(2,1)S(1)}, u32[]{:S(2)}, u32[]{:S(2)}) collective-permute-start(bf16[256,512]{1,0:T(8,128)(2,1)S(1)} %copy-done.2), channel_id=1, source_target_pairs={{6,4},{7,5},{14,12},{15,13},{22,20},{23,21},{30,28},{31,29}} | collective-permute-start | bytes 786440 | tf_op jit(solution)/shard_map/ppermute | solution.py:301
  55.2 8.0 %collective-permute-start.10 = (bf16[256,512]{1,0:T(8,128)(2,1)S(1)}, bf16[256,512]{1,0:T(8,128)(2,1)S(1)}, u32[]{:S(2)}, u32[]{:S(2)}) collective-permute-start(bf16[256,512]{1,0:T(8,128)(2,1)S(1)} %get-tuple-element.37), channel_id=1, source_target_pairs={{4,0},{5,1},{6,2},{7,3},{12,8},{13,9},{14,10},{15,11},{20,16},{21,... | collective-permute-start | bytes 786440 | tf_op jit(solution)/shard_map/ppermute | solution.py:301
  63.3 10.4 %collective-permute-start.11 = (bf16[128,512]{1,0:T(8,128)(2,1)S(1)}, bf16[128,512]{1,0:T(8,128)(2,1)S(1)}, u32[]{:S(2)}, u32[]{:S(2)}) collective-permute-start(bf16[128,512]{1,0:T(8,128)(2,1)S(1)} %get-tuple-element.35), channel_id=1, source_target_pairs={{0,24},{1,25},{2,26},{3,27},{4,28},{5,29},{6,30},{7,31},{8,0},{9,1... | collective-permute-start | bytes 393224 | tf_op jit(solution)/shard_map/ppermute | solution.py:250
  69.7 6.1 %collective-permute-start.12 = (bf16[128,512]{1,0:T(8,128)(2,1)S(1)}, bf16[128,512]{1,0:T(8,128)(2,1)S(1)}, u32[]{:S(2)}, u32[]{:S(2)}) collective-permute-start(bf16[128,512]{1,0:T(8,128)(2,1)S(1)} %get-tuple-element.36), channel_id=1, source_target_pairs={{0,25},{1,24},{2,27},{3,26},{4,29},{5,28},{6,31},{7,30},{8,1},{9,0... | collective-permute-start | bytes 393224 | tf_op jit(solution)/shard_map/ppermute | solution.py:250

commit v3 on v2

--- a/solution.py
+++ b/solution.py
@@ -19,7 +19,6 @@
 WIDE = GROUP * HEAD_SIZE
 PAIR = 2 * HEAD_SIZE
 MASKED = -1e30
-NONE, WHOLE, CAUSAL = 0, 1, 2
 
 SCALE = 1.0 / math.sqrt(HEAD_SIZE)
 FACTOR = SCALE / math.log(2.0)
@@ -32,19 +31,22 @@
 
 
 def attention_kernel(levels, *refs):
-    place_ref, mode_ref, side_ref, segs_ref = refs[:4]
+    list_ref, count_ref, where_ref, segs_ref, told_ref = refs[:5]
+    refs = refs[1:]
     query_ref, grad_ref, partner_ref = refs[4:7]
     held = refs[7 : 7 + levels][::-1]
     outs = refs[7 + levels : 9 + levels]
     term_refs = refs[9 + levels : 9 + 2 * levels]
     scratch = refs[9 + 2 * levels :]
     rows_of = [pl.ds(2 * j * BLOCK, 2 * BLOCK) for j in range(levels - 1)]
-    rows_of.append(pl.ds(pl.multiple_of(2 * side_ref[1] * BLOCK, 2 * BLOCK), 2 * BLOCK))
+    rows_of.append(pl.ds(pl.multiple_of(2 * where_ref[1] * BLOCK, 2 * BLOCK), 2 * BLOCK))
     kv, rows_in, rows_out, bias, probs, dscores, sums = scratch[:7]
     terms = scratch[7 : 7 + levels]
     arrived, left = scratch[-2:]
 
-    first_col = side_ref[0] * HALF_Q
+    mine = where_ref[0]
+    side = mine & 1
+    first_col = side * HALF_Q
     arrivals = []
     for group in range(HALF_KV):
         at = pl.ds(group * PAIR, PAIR)
@@ -81,25 +83,35 @@
 
     key_at = lax.broadcasted_iota(jnp.int32, (BLOCK, BLOCK), 0)
     query_at = lax.broadcasted_iota(jnp.int32, (BLOCK, BLOCK), 1)
+    told_list = told_ref[:, BLOCK : BLOCK + LIST + 1].astype(jnp.float32)
+    lane = lax.broadcasted_iota(jnp.int32, told_list.shape, 1)
+
+    def told_number(i):
+        return jnp.sum(jnp.where(lane == i, told_list, 0.0)).astype(jnp.int32)
+
     shifts = []
     places = []
     for block in range(2):
-        seg_of_query = jnp.broadcast_to(segs_ref[block : block + 1, :], (BLOCK, BLOCK))
+        if block == 0:
+            segs = segs_ref[...]
+            listed = [list_ref[slot] for slot in range(LIST)]
+            count = count_ref[0]
+        else:
+            segs = told_ref[:, :BLOCK]
+            listed = [told_number(slot) for slot in range(LIST)]
+            count = told_number(LIST)
+        here = mine ^ block
+        seg_of_query = jnp.broadcast_to(segs, (BLOCK, BLOCK))
         causal = (key_at <= query_at) & (seg_of_query.T == seg_of_query)
-        mode = mode_ref[block * LIST]
-        bias[block] = jnp.where((mode == CAUSAL) & causal, 0.0, MASKED)
-        shifts.append(
-            [
-                jnp.where(mode_ref[block * LIST + slot] == WHOLE, 0.0, -MASKED)
-                for slot in range(1, LIST)
-            ]
-        )
-        places.append(
-            [
-                pl.ds(pl.multiple_of(place_ref[block * LIST + slot] * BLOCK, BLOCK), BLOCK)
-                for slot in range(LIST)
-            ]
-        )
+        bias[block] = jnp.where(causal, 0.0, MASKED)
+        whole = [(slot < count) & (listed[slot] < here) for slot in range(LIST)]
+        shifts.append([jnp.where(whole[slot], 0.0, -MASKED) for slot in range(1, LIST)])
+        spots = []
+        for slot in range(LIST):
+            shown = jnp.where(whole[slot], listed[slot], here)
+            spot = 2 * ((mine >> 1) - (shown >> 1)) + ((shown & 1) ^ side)
+            spots.append(pl.ds(pl.multiple_of(spot * BLOCK, BLOCK), BLOCK))
+        places.append(spots)
 
     departures = []
 
@@ -188,7 +200,7 @@
         copy.wait()
 
 
-def attention(levels, place, mode, side, segs, queries, grads, partner, held):
+def attention(levels, lists, count, where, segs, told, queries, grads, partner, held):
     smem = pl.BlockSpec(memory_space=pltpu.SMEM)
     anywhere = pl.BlockSpec(memory_space=pl.ANY)
     keys = LIST * BLOCK
@@ -203,7 +215,9 @@
     return pl.pallas_call(
         lambda *refs: attention_kernel(levels, *refs),
         out_shape=outs + terms,
-        in_specs=[smem, smem, smem, pl.BlockSpec(memory_space=pltpu.VMEM)]
+        in_specs=[smem, smem, smem, pl.BlockSpec(memory_space=pltpu.VMEM)] + [
+            pl.BlockSpec(memory_space=pltpu.VMEM)
+        ]
         + [anywhere] * (3 + levels),
         out_specs=[anywhere] * (2 + levels),
         scratch_shapes=[
@@ -226,7 +240,7 @@
             bytes_accessed=8 * 1024 * 1024,
             transcendentals=keys * BLOCK * QUERY_HEADS,
         ),
-    )(place, mode, side, segs, queries, grads, partner, *held[::-1])
+    )(lists, count, where, segs, told, queries, grads, partner, *held[::-1])
 
 
 def per_device(
@@ -260,36 +274,26 @@
         return jnp.concatenate(parts, axis=1)
 
     facts = jnp.concatenate([segment_ids[0], block_lists[0, 0], list_counts[0]])[None]
-    facts_got = lax.ppermute(facts, "blk", swap)
+    told = lax.ppermute(facts, "blk", swap)
     other = lax.ppermute(heads_of(1 - side), "blk", swap)
     theirs = jnp.concatenate(
         [columns(a, (1 - side) * HALF_Q, HALF_Q) for a in (queries, out_grads)], axis=1
     )
-    theirs, other, facts_got = lax.optimization_barrier((theirs, other, facts_got))
+    theirs, other = lax.optimization_barrier((theirs, other))
     partner = lax.ppermute(theirs, "blk", swap)
     held = [jnp.concatenate([heads_of(side), other], axis=0)]
     for hop in range(1, levels):
         pairs = [(i, i + 2 * hop) for i in range(blocks - 2 * hop)]
         held.append(lax.ppermute(held[0], "blk", pairs))
 
-    facts = jnp.concatenate([facts, facts_got], axis=0)
-    segs = facts[:, :BLOCK]
-    lists = facts[:, BLOCK : BLOCK + LIST]
-    counts = facts[:, BLOCK + LIST :]
-    block = jnp.stack([mine, mine ^ 1])[:, None].astype(jnp.int32)
-    listed = jnp.arange(LIST, dtype=jnp.int32)[None, :] < counts
-    mode = jnp.where(lists == block, CAUSAL, jnp.where(lists < block, WHOLE, NONE))
-    mode = jnp.where(listed, mode, NONE).astype(jnp.int32)
-    place = 2 * (level - lists // 2) + (lists % 2 != side).astype(jnp.int32)
-    place = jnp.where(mode == NONE, 0, place).astype(jnp.int32)
-
     top = levels - 1
     own_out, partner_out, here, near, *between, first = attention(
         levels,
-        place.reshape(-1),
-        mode.reshape(-1),
-        jnp.stack([side, jnp.where(level == top, top, 1)]).astype(jnp.int32),
-        segs,
+        block_lists[0, 0],
+        list_counts[0],
+        jnp.stack([mine, jnp.where(level == top, top, 1)]).astype(jnp.int32),
+        segment_ids,
+        told,
         queries[0],
         out_grads[0],
         partner,

time: 78.6 us -> 76.9 us (0.978)
  other arithmetic: 6.44 us -> 4.92 us
  local copies, waits for them, and re-layouts: 4.45 us -> 3.46 us
    ppermute x1, waiting for transfers between devices: 0.01 us -> 11.9 us  [per_device(): told = lax.ppermute(facts, 'blk', swap)]
    ppermute x3, waiting for transfers between devices: 8.04 us -> 0.01 us  [per_device(): held.append(lax.ppermute(held[0], 'blk', pairs))]
    ppermute x1, waiting for transfers between devices: 2.73 us -> 0.01 us  [per_device(): partner = lax.ppermute(theirs, 'blk', swap)]
    ppermute x1, starting transfers between devices: 0.07 us -> 2.13 us  [per_device(): other = lax.ppermute(heads_of(1 - side), 'blk', swap)]
    ppermute x1, starting transfers between devices: 2.07 us -> 0.23 us  [per_device(): told = lax.ppermute(facts, 'blk', swap)]
    reshape x2 -> x0, local copies, waits for them, and re-layouts: 1.22 us -> none  [the longest x1 0.65 us: per_device(): mode.reshape(-1)]
    ppermute x4, starting transfers between devices: 11.2 us -> 10.2 us  [back(): return lax.ppermute(value, ('section', 'blk'), pairs)]
  transfers between devices with their start and end apart: 13 -> 13, of which waited for: 8 -> 6; matrix products, arithmetic and copies ran while one was open for 10% -> 6% of each run, Pallas kernels for 0% -> 0%
where the time goes in v3:
time: 76.9 us; the launch traced here: 75.6 us
  waiting for transfers between devices  28.5 us (37%)
  starting transfers between devices  25.7 us (33%)
  Pallas kernels  11.4 us (15%)
  other arithmetic  4.92 us (6%)
  local copies, waits for them, and re-layouts  3.46 us (4%)
  between operations  1.55 us (2%)
    ppermute x1, waiting for transfers between devices, per_device(): told = lax.ppermute(facts, 'blk', swap)  11.9 us
    pallas_call x1, Pallas kernels, attention(): pl.pallas_call(lambda *refs: attention_kernel(levels, *refs), out_shape=o...  11.4 us
    ppermute x3, waiting for transfers between devices, down(): return lax.ppermute(terms, 'blk', pairs)  11 us
    ppermute x4, starting transfers between devices, back(): return lax.ppermute(value, ('section', 'blk'), pairs)  10.2 us
    ppermute x3, starting transfers between devices, per_device(): held.append(lax.ppermute(held[0], 'blk', pairs))  8.74 us
    ppermute x4, waiting for transfers between devices, back(): return lax.ppermute(value, ('section', 'blk'), pairs)  3.87 us
    ppermute x3, starting transfers between devices, down(): return lax.ppermute(terms, 'blk', pairs)  3.26 us
    select_n x3, other arithmetic, ordered(): jnp.where(side == 0, jnp.concatenate([a, b], axis=1), jnp.concatenate([b,...  2.59 us
  transfers between devices with their start and end apart: 13, of which 6 were waited for; matrix products, arithmetic and copies ran while one was open for 6% of the time, Pallas kernels for 0%

profile of v3, /device:TPU:1, one launch (start us, length us, event | category | flops | bytes accessed | tf_op | source)
XLA Modules:
  0.0 75.6 jit_solution(2707993960080528771)
XLA Ops:
  0.7 0.9 %dynamic-slice_bitcast_fusion.4 = (bf16[128,128]{1,0:T(8,128)(2,1)S(1)}, bf16[128,128]{1,0:T(8,128)(2,1)S(1)}, bf16[128,128]{1,0:T(8,128)(2,1)S(1)}, bf16[128,12...) fusion(bf16[1,128,512]{2,1,0:T(8,128)(2,1)} %param.9, ...), kind=kLoop, calls=%fused_computation.23 | loop fusion | bytes 524304 | tf_op jit(solution)/shard_map/dynamic_slice | solution.py:267
  1.6 2.1 %collective-permute-start.1 = (bf16[128,512]{1,0:T(8,128)(2,1)S(1)}, bf16[128,512]{1,0:T(8,128)(2,1)S(1)}, u32[]{:S(2)}, u32[]{:S(2)}) collective-permute-start(bf16[128,512]{1,0:T(8,128)(2,1)S(1)} %pad_maximum_fusion.2), channel_id=1, source_target_pairs={{0,1},{1,0},{2,3},{3,2},{4,5},{5,4},{6,7},{7,6},{8,9},{9,8},{10,11... | collective-permute-start | bytes 393224 | tf_op jit(solution)/shard_map/ppermute | solution.py:278
  3.7 1.3 %dynamic-slice_bitcast_fusion = (bf16[128,2048]{1,0:T(8,128)(2,1)S(1)}, bf16[128,2048]{1,0:T(8,128)(2,1)S(1)}) fusion(bf16[1,128,4096]{2,1,0:T(8,128)(2,1)} %param.10, s32[]{:T(128)S(6)} %select_n.88, bf16[1,128,4096]{2,1,0:T(8,128)(2,1)} %param.7), kind=kLoop, calls=%fused_computation.7 | loop fusion | bytes 2097156 | tf_op jit(solution)/shard_map/dynamic_slice | solution.py:267
  5.1 1.8 %collective-permute-done.1 = bf16[128,512]{1,0:T(8,128)(2,1)S(1)} collective-permute-done((bf16[128,512]{1,0:T(8,128)(2,1)S(1)}, bf16[128,512]{1,0:T(8,128)(2,1)S(1)}, u32[]{:S(2)}, u32[]{:S(2)}) %collective-permute-start.1) | collective-permute-done | bytes 131104 | tf_op jit(solution)/shard_map/ppermute | solution.py:278
  7.0 1.1 %collective-permute-start.2 = (bf16[128,4096]{1,0:T(8,128)(2,1)S(1)}, bf16[128,4096]{1,0:T(8,128)(2,1)S(1)}, u32[]{:S(2)}, u32[]{:S(2)}) collective-permute-start(bf16[128,4096]{1,0:T(8,128)(2,1)S(1)} %pad_maximum_fusion), channel_id=1, source_target_pairs={{0,1},{1,0},{2,3},{3,2},{4,5},{5,4},{6,7},{7,6},{8,9},{9,8},{10,11... | collective-permute-start | bytes 3145736 | tf_op jit(solution)/shard_map/ppermute | solution.py:283
  8.1 3.2 %collective-permute-start.5 = (bf16[256,512]{1,0:T(8,128)(2,1)S(1)}, bf16[256,512]{1,0:T(8,128)(2,1)S(1)}, u32[]{:S(2)}, u32[]{:S(2)}) collective-permute-start(bf16[256,512]{1,0:T(8,128)(2,1)S(1)} %pad_maximum_fusion.1.refs_11_), channel_id=1, source_target_pairs={{0,2},{1,3},{2,4},{3,5},{4,6},{5,7},{8,10},{9,11},{10,12},{11,13},... | collective-permute-start | bytes 786440 | tf_op jit(solution)/shard_map/ppermute | solution.py:287
  11.4 4.2 %collective-permute-start.4 = (bf16[256,512]{1,0:T(8,128)(2,1)S(1)}, bf16[256,512]{1,0:T(8,128)(2,1)S(1)}, u32[]{:S(2)}, u32[]{:S(2)}) collective-permute-start(bf16[256,512]{1,0:T(8,128)(2,1)S(1)} %pad_maximum_fusion.1.refs_11_), channel_id=1, source_target_pairs={{0,4},{1,5},{2,6},{3,7},{8,12},{9,13},{10,14},{11,15},{16,20},{17,... | collective-permute-start | bytes 786440 | tf_op jit(solution)/shard_map/ppermute | solution.py:287
  15.6 1.3 %collective-permute-start.3 = (bf16[256,512]{1,0:T(8,128)(2,1)S(1)}, bf16[256,512]{1,0:T(8,128)(2,1)S(1)}, u32[]{:S(2)}, u32[]{:S(2)}) collective-permute-start(bf16[256,512]{1,0:T(8,128)(2,1)S(1)} %pad_maximum_fusion.1.refs_11_), channel_id=1, source_target_pairs={{0,6},{1,7},{8,14},{9,15},{16,22},{17,23},{24,30},{25,31}} | collective-permute-start | bytes 786440 | tf_op jit(solution)/shard_map/ppermute | solution.py:287
  17.6 0.2 collective-permute-start
  17.9 0.7 pad_add_fusion.1.refs_2_
  18.5 11.9 %collective-permute-done.refs_4_ = s32[1,133]{1,0:T(1,128)S(1)} collective-permute-done((s32[1,133]{1,0:T(1,128)S(1)}, s32[1,133]{1,0:T(1,128)S(1)}, u32[]{:S(2)}, u32[]{:S(2)}) %collective-permute-start) | collective-permute-done | bytes 564 | tf_op jit(solution)/shard_map/ppermute | solution.py:277
  30.5 0.5 copy-done.8
  31.0 0.2 copy-done.4
  31.2 0.1 copy-done.6
  31.3 0.4 copy-done.3
  31.6 11.4 %shard_map.94 = (bf16[128,2048]{1,0:T(8,128)(2,1)}, bf16[128,2048]{1,0:T(8,128)(2,1)}, f32[256,512]{1,0:T(8,128)}, bf16[256,512]{1,0:T(8,128)(2,1)}, f32[256,512]{1,0:T(8,128)}, /*index=5*/bf16[256,512]{1,0:T(8,128)(2,1)}) custom-call(s32[4]{0:T(128)} %bitcast.53, s32[1]{0:T(128)} %bitcast.47.refs_1_, s32[2]{0:T(128)} %pad_add_fusion.1.refs_2_, ...), custom_call_target="tpu_custom_call" | custom-call | flops 2684354560 | bytes 8388608 | tf_op jit(solution)/shard_map/pallas_call | solution.py:215
  43.0 1.3 %collective-permute-start.6 = (bf16[256,512]{1,0:T(8,128)(2,1)}, bf16[256,512]{1,0:T(8,128)(2,1)S(1)}, u32[]{:S(2)}, u32[]{:S(2)}) collective-permute-start(bf16[256,512]{1,0:T(8,128)(2,1)} %get-tuple-element.21), channel_id=1, source_target_pairs={{2,0},{3,1},{4,2},{5,3},{6,4},{7,5},{10,8},{11,9},{12,10},{13,11},... | collective-permute-start | bytes 786440 | tf_op jit(solution)/shard_map/ppermute | solution.py:305
  44.3 2.2 %collective-permute-start.8 = (bf16[128,2048]{1,0:T(8,128)(2,1)}, bf16[128,2048]{1,0:T(8,128)(2,1)S(1)}, u32[]{:S(2)}, u32[]{:S(2)}) collective-permute-start(bf16[128,2048]{1,0:T(8,128)(2,1)} %get-tuple-element.23), channel_id=1, source_target_pairs={{0,24},{1,25},{2,26},{3,27},{4,28},{5,29},{6,30},{7,31},{8,0},{9,1... | collective-permute-start | bytes 1572872 | tf_op jit(solution)/shard_map/ppermute | solution.py:264
  46.6 1.1 %collective-permute-start.9 = (bf16[128,2048]{1,0:T(8,128)(2,1)}, bf16[128,2048]{1,0:T(8,128)(2,1)S(1)}, u32[]{:S(2)}, u32[]{:S(2)}) collective-permute-start(bf16[128,2048]{1,0:T(8,128)(2,1)} %get-tuple-element.24), channel_id=1, source_target_pairs={{0,25},{1,24},{2,27},{3,26},{4,29},{5,28},{6,31},{7,30},{8,1},{9,0... | collective-permute-start | bytes 1572872 | tf_op jit(solution)/shard_map/ppermute | solution.py:264
  47.7 4.3 %collective-permute-done.6 = bf16[256,512]{1,0:T(8,128)(2,1)S(1)} collective-permute-done((bf16[256,512]{1,0:T(8,128)(2,1)}, bf16[256,512]{1,0:T(8,128)(2,1)S(1)}, u32[]{:S(2)}, u32[]{:S(2)}) %collective-permute-start.6) | collective-permute-done | bytes 262176 | tf_op jit(solution)/shard_map/ppermute | solution.py:305
  52.0 1.4 %fusion.1 = (bf16[256,512]{1,0:T(8,128)(2,1)S(1)}, f32[256,512]{1,0:T(8,128)S(1)}) fusion(f32[256,512]{1,0:T(8,128)} %get-tuple-element.25, bf16[256,512]{1,0:T(8,128)(2,1)S(1)} %collective-permute-done.6, f32[256,512]{1,0:T(8,128)} %get-tuple-element.20, pred[]{:T(512)S(6)} %eq.15), kind=kLoop, calls=%fused_computation.5 | loop fusion | flops 655360 | bytes 2097153 | tf_op jit(solution)/shard_map/convert_element_type | solution.py:312
  53.4 0.7 collective-permute-start.7
  54.0 1.3 %collective-permute-start.10 = (bf16[256,512]{1,0:T(8,128)(2,1)S(1)}, bf16[256,512]{1,0:T(8,128)(2,1)S(1)}, u32[]{:S(2)}, u32[]{:S(2)}) collective-permute-start(bf16[256,512]{1,0:T(8,128)(2,1)S(1)} %get-tuple-element.33), channel_id=1, source_target_pairs={{4,0},{5,1},{6,2},{7,3},{12,8},{13,9},{14,10},{15,11},{20,16},{21,... | collective-permute-start | bytes 786440 | tf_op jit(solution)/shard_map/ppermute | solution.py:305
  55.4 6.7 %collective-permute-done.10 = bf16[256,512]{1,0:T(8,128)(2,1)S(1)} collective-permute-done((bf16[256,512]{1,0:T(8,128)(2,1)S(1)}, bf16[256,512]{1,0:T(8,128)(2,1)S(1)}, u32[]{:S(2)}, u32[]{:S(2)}) %collective-permute-start.10) | collective-permute-done | bytes 262176 | tf_op jit(solution)/shard_map/ppermute | solution.py:305
  62.1 0.1 add_convert_fusion
  62.2 6.7 %collective-permute-start.11 = (bf16[128,512]{1,0:T(8,128)(2,1)S(1)}, bf16[128,512]{1,0:T(8,128)(2,1)S(1)}, u32[]{:S(2)}, u32[]{:S(2)}) collective-permute-start(bf16[128,512]{1,0:T(8,128)(2,1)S(1)} %get-tuple-element.31), channel_id=1, source_target_pairs={{0,24},{1,25},{2,26},{3,27},{4,28},{5,29},{6,30},{7,31},{8,0},{9,1... | collective-permute-start | bytes 393224 | tf_op jit(solution)/shard_map/ppermute | solution.py:264
  68.9 0.2 collective-permute-start.12
  69.1 1.2 %maximum_select_fusion = bf16[1,128,4096]{2,1,0:T(8,128)(2,1)} fusion(bf16[1,128,2048]{2,1,0:T(8,128)(2,1)S(1)} %bitcast.49, bf16[1,128,2048]{2,1,0:T(8,128)(2,1)S(1)} %bitcast.48, pred[]{:T(512)S(6)} %eq.13), kind=kLoop, calls=%fused_computation.1 | loop fusion | flops 4718592 | bytes 2097153 | tf_op jit(solution)/shard_map/jit(_where)/select_n | solution.py:322
  70.3 2.6 %collective-permute-done.11 = bf16[128,512]{1,0:T(8,128)(2,1)S(1)} collective-permute-done((bf16[128,512]{1,0:T(8,128)(2,1)S(1)}, bf16[128,512]{1,0:T(8,128)(2,1)S(1)}, u32[]{:S(2)}, u32[]{:S(2)}) %collective-permute-start.11) | collective-permute-done | bytes 131104 | tf_op jit(solution)/shard_map/ppermute | solution.py:264
  72.9 1.2 %collective-permute-done.12 = bf16[128,512]{1,0:T(8,128)(2,1)S(1)} collective-permute-done((bf16[128,512]{1,0:T(8,128)(2,1)S(1)}, bf16[128,512]{1,0:T(8,128)(2,1)S(1)}, u32[]{:S(2)}, u32[]{:S(2)}) %collective-permute-start.12) | collective-permute-done | bytes 131104 | tf_op jit(solution)/shard_map/ppermute | solution.py:264
  74.2 0.7 maximum_select_fusion.2
  74.9 0.7 maximum_select_fusion.1
  (28 shorter events, 0.4 us)
Async XLA Ops:
  1.6 5.4 %collective-permute-start.1 = (bf16[128,512]{1,0:T(8,128)(2,1)S(1)}, bf16[128,512]{1,0:T(8,128)(2,1)S(1)}, u32[]{:S(2)}, u32[]{:S(2)}) collective-permute-start(bf16[128,512]{1,0:T(8,128)(2,1)S(1)} %pad_maximum_fusion.2), channel_id=1, source_target_pairs={{0,1},{1,0},{2,3},{3,2},{4,5},{5,4},{6,7},{7,6},{8,9},{9,8},{10,11... | collective-permute-start | bytes 393224 | tf_op jit(solution)/shard_map/ppermute | solution.py:278
  5.0 12.5 %copy-start.1 = (s32[1,1,4]{2,1,0:T(1,128)S(1)}, s32[1,1,4]{2,1,0:T(1,128)}, u32[]{:S(2)}) copy-start(s32[1,1,4]{2,1,0:T(1,128)} %param.12) | copy-start | bytes 52
  5.1 12.5 %copy-start.2 = (s32[1,128]{1,0:T(1,128)S(1)}, s32[1,128]{1,0:T(1,128)}, u32[]{:S(2)}) copy-start(s32[1,128]{1,0:T(1,128)} %refs_3_.1) | copy-start | bytes 1540
  7.0 23.5 %collective-permute-start.2 = (bf16[128,4096]{1,0:T(8,128)(2,1)S(1)}, bf16[128,4096]{1,0:T(8,128)(2,1)S(1)}, u32[]{:S(2)}, u32[]{:S(2)}) collective-permute-start(bf16[128,4096]{1,0:T(8,128)(2,1)S(1)} %pad_maximum_fusion), channel_id=1, source_target_pairs={{0,1},{1,0},{2,3},{3,2},{4,5},{5,4},{6,7},{7,6},{8,9},{9,8},{10,11... | collective-permute-start | bytes 3145736 | tf_op jit(solution)/shard_map/ppermute | solution.py:283
  8.1 22.3 %copy-start = (bf16[256,512]{1,0:T(8,128)(2,1)}, bf16[256,512]{1,0:T(8,128)(2,1)S(1)}, u32[]{:S(2)}) copy-start(bf16[256,512]{1,0:T(8,128)(2,1)S(1)} %pad_maximum_fusion.1.refs_11_) | copy-start | bytes 786436
  8.1 22.3 %collective-permute-start.5 = (bf16[256,512]{1,0:T(8,128)(2,1)S(1)}, bf16[256,512]{1,0:T(8,128)(2,1)S(1)}, u32[]{:S(2)}, u32[]{:S(2)}) collective-permute-start(bf16[256,512]{1,0:T(8,128)(2,1)S(1)} %pad_maximum_fusion.1.refs_11_), channel_id=1, source_target_pairs={{0,2},{1,3},{2,4},{3,5},{4,6},{5,7},{8,10},{9,11},{10,12},{11,13},... | collective-permute-start | bytes 786440 | tf_op jit(solution)/shard_map/ppermute | solution.py:287
  11.4 19.0 %collective-permute-start.4 = (bf16[256,512]{1,0:T(8,128)(2,1)S(1)}, bf16[256,512]{1,0:T(8,128)(2,1)S(1)}, u32[]{:S(2)}, u32[]{:S(2)}) collective-permute-start(bf16[256,512]{1,0:T(8,128)(2,1)S(1)} %pad_maximum_fusion.1.refs_11_), channel_id=1, source_target_pairs={{0,4},{1,5},{2,6},{3,7},{8,12},{9,13},{10,14},{11,15},{16,20},{17,... | collective-permute-start | bytes 786440 | tf_op jit(solution)/shard_map/ppermute | solution.py:287
  15.6 14.8 %collective-permute-start.3 = (bf16[256,512]{1,0:T(8,128)(2,1)S(1)}, bf16[256,512]{1,0:T(8,128)(2,1)S(1)}, u32[]{:S(2)}, u32[]{:S(2)}) collective-permute-start(bf16[256,512]{1,0:T(8,128)(2,1)S(1)} %pad_maximum_fusion.1.refs_11_), channel_id=1, source_target_pairs={{0,6},{1,7},{8,14},{9,15},{16,22},{17,23},{24,30},{25,31}} | collective-permute-start | bytes 786440 | tf_op jit(solution)/shard_map/ppermute | solution.py:287
  17.6 12.8 %collective-permute-start = (s32[1,133]{1,0:T(1,128)S(1)}, s32[1,133]{1,0:T(1,128)S(1)}, u32[]{:S(2)}, u32[]{:S(2)}) collective-permute-start(s32[1,133]{1,0:T(1,128)S(1)} %bitcast.52), channel_id=1, source_target_pairs={{0,1},{1,0},{2,3},{3,2},{4,5},{5,4},{6,7},{7,6},{8,9},{9,8},{10,11... | collective-permute-start | bytes 1604 | tf_op jit(solution)/shard_map/ppermute | solution.py:277
  30.4 0.6 copy-start.8
  30.4 0.7 copy-start.4
  30.4 0.8 %copy-start.5 = (bf16[256,512]{1,0:T(8,128)(2,1)}, bf16[256,512]{1,0:T(8,128)(2,1)S(1)}, u32[]{:S(2)}) copy-start(bf16[256,512]{1,0:T(8,128)(2,1)S(1)} %collective-permute-done.4.refs_9_) | copy-start | bytes 786436
  30.4 0.8 %copy-start.6 = (bf16[256,512]{1,0:T(8,128)(2,1)}, bf16[256,512]{1,0:T(8,128)(2,1)S(1)}, u32[]{:S(2)}) copy-start(bf16[256,512]{1,0:T(8,128)(2,1)S(1)} %collective-permute-done.3.refs_8_) | copy-start | bytes 786436
  30.5 1.2 %copy-start.3 = (bf16[128,4096]{1,0:T(8,128)(2,1)}, bf16[128,4096]{1,0:T(8,128)(2,1)S(1)}, u32[]{:S(2)}) copy-start(bf16[128,4096]{1,0:T(8,128)(2,1)S(1)} %collective-permute-done.2.refs_7_) | copy-start | bytes 3145732
  43.0 8.9 %collective-permute-start.6 = (bf16[256,512]{1,0:T(8,128)(2,1)}, bf16[256,512]{1,0:T(8,128)(2,1)S(1)}, u32[]{:S(2)}, u32[]{:S(2)}) collective-permute-start(bf16[256,512]{1,0:T(8,128)(2,1)} %get-tuple-element.21), channel_id=1, source_target_pairs={{2,0},{3,1},{4,2},{5,3},{6,4},{7,5},{10,8},{11,9},{12,10},{13,11},... | collective-permute-start | bytes 786440 | tf_op jit(solution)/shard_map/ppermute | solution.py:305
  44.3 17.7 %collective-permute-start.8 = (bf16[128,2048]{1,0:T(8,128)(2,1)}, bf16[128,2048]{1,0:T(8,128)(2,1)S(1)}, u32[]{:S(2)}, u32[]{:S(2)}) collective-permute-start(bf16[128,2048]{1,0:T(8,128)(2,1)} %get-tuple-element.23), channel_id=1, source_target_pairs={{0,24},{1,25},{2,26},{3,27},{4,28},{5,29},{6,30},{7,31},{8,0},{9,1... | collective-permute-start | bytes 1572872 | tf_op jit(solution)/shard_map/ppermute | solution.py:264
  46.6 15.5 %collective-permute-start.9 = (bf16[128,2048]{1,0:T(8,128)(2,1)}, bf16[128,2048]{1,0:T(8,128)(2,1)S(1)}, u32[]{:S(2)}, u32[]{:S(2)}) collective-permute-start(bf16[128,2048]{1,0:T(8,128)(2,1)} %get-tuple-element.24), channel_id=1, source_target_pairs={{0,25},{1,24},{2,27},{3,26},{4,29},{5,28},{6,31},{7,30},{8,1},{9,0... | collective-permute-start | bytes 1572872 | tf_op jit(solution)/shard_map/ppermute | solution.py:264
  52.0 1.4 %copy-start.7 = (bf16[256,512]{1,0:T(8,128)(2,1)S(1)}, bf16[256,512]{1,0:T(8,128)(2,1)}, u32[]{:S(2)}) copy-start(bf16[256,512]{1,0:T(8,128)(2,1)} %get-tuple-element.22) | copy-start | bytes 786436
  53.4 2.0 %collective-permute-start.7 = (bf16[256,512]{1,0:T(8,128)(2,1)S(1)}, bf16[256,512]{1,0:T(8,128)(2,1)S(1)}, u32[]{:S(2)}, u32[]{:S(2)}) collective-permute-start(bf16[256,512]{1,0:T(8,128)(2,1)S(1)} %copy-done.7), channel_id=1, source_target_pairs={{6,4},{7,5},{14,12},{15,13},{22,20},{23,21},{30,28},{31,29}} | collective-permute-start | bytes 786440 | tf_op jit(solution)/shard_map/ppermute | solution.py:305
  54.0 8.0 %collective-permute-start.10 = (bf16[256,512]{1,0:T(8,128)(2,1)S(1)}, bf16[256,512]{1,0:T(8,128)(2,1)S(1)}, u32[]{:S(2)}, u32[]{:S(2)}) collective-permute-start(bf16[256,512]{1,0:T(8,128)(2,1)S(1)} %get-tuple-element.33), channel_id=1, source_target_pairs={{4,0},{5,1},{6,2},{7,3},{12,8},{13,9},{14,10},{15,11},{20,16},{21,... | collective-permute-start | bytes 786440 | tf_op jit(solution)/shard_map/ppermute | solution.py:305
  62.2 10.7 %collective-permute-start.11 = (bf16[128,512]{1,0:T(8,128)(2,1)S(1)}, bf16[128,512]{1,0:T(8,128)(2,1)S(1)}, u32[]{:S(2)}, u32[]{:S(2)}) collective-permute-start(bf16[128,512]{1,0:T(8,128)(2,1)S(1)} %get-tuple-element.31), channel_id=1, source_target_pairs={{0,24},{1,25},{2,26},{3,27},{4,28},{5,29},{6,30},{7,31},{8,0},{9,1... | collective-permute-start | bytes 393224 | tf_op jit(solution)/shard_map/ppermute | solution.py:264
  68.9 5.3 %collective-permute-start.12 = (bf16[128,512]{1,0:T(8,128)(2,1)S(1)}, bf16[128,512]{1,0:T(8,128)(2,1)S(1)}, u32[]{:S(2)}, u32[]{:S(2)}) collective-permute-start(bf16[128,512]{1,0:T(8,128)(2,1)S(1)} %get-tuple-element.32), channel_id=1, source_target_pairs={{0,25},{1,24},{2,27},{3,26},{4,29},{5,28},{6,31},{7,30},{8,1},{9,0... | collective-permute-start | bytes 393224 | tf_op jit(solution)/shard_map/ppermute | solution.py:264

commit v4 on v3

--- a/solution.py
+++ b/solution.py
@@ -36,12 +36,13 @@
     query_ref, grad_ref, partner_ref = refs[4:7]
     held = refs[7 : 7 + levels][::-1]
     outs = refs[7 + levels : 9 + levels]
-    term_refs = refs[9 + levels : 9 + 2 * levels]
-    scratch = refs[9 + 2 * levels :]
+    term_refs = refs[9 + levels : 10 + 2 * levels]
+    scratch = refs[10 + 2 * levels :]
     rows_of = [pl.ds(2 * j * BLOCK, 2 * BLOCK) for j in range(levels - 1)]
     rows_of.append(pl.ds(pl.multiple_of(2 * where_ref[1] * BLOCK, 2 * BLOCK), 2 * BLOCK))
+    rows_of.append(rows_of[2])
     kv, rows_in, rows_out, bias, probs, dscores, sums = scratch[:7]
-    terms = scratch[7 : 7 + levels]
+    terms = scratch[7 : 8 + levels]
     arrived, left = scratch[-2:]
 
     mine = where_ref[0]
@@ -192,7 +193,7 @@
                 sums[places[block][slot], key_cols] += key_terms[at]
                 sums[places[block][slot], value_cols] += value_terms[at]
         cols = slice(group * PAIR, (group + 1) * PAIR)
-        for j in range(levels):
+        for j in range(levels + 1):
             terms[j][:, cols] = sums[rows_of[j], cols].astype(terms[j].dtype)
             cut = pl.ds(group * PAIR, PAIR)
             send(terms[j].at[:, cut], term_refs[j].at[:, cut])
@@ -208,9 +209,9 @@
     outs = [jax.ShapeDtypeStruct((BLOCK, HALF_Q), jnp.bfloat16)] * 2
     terms = [
         jax.ShapeDtypeStruct(
-            (2 * BLOCK, width), jnp.bfloat16 if j in (1, levels - 1) else jnp.float32
+            (2 * BLOCK, width), jnp.bfloat16 if j in (1, levels - 1, levels) else jnp.float32
         )
-        for j in range(levels)
+        for j in range(levels + 1)
     ]
     return pl.pallas_call(
         lambda *refs: attention_kernel(levels, *refs),
@@ -219,7 +220,7 @@
             pl.BlockSpec(memory_space=pltpu.VMEM)
         ]
         + [anywhere] * (3 + levels),
-        out_specs=[anywhere] * (2 + levels),
+        out_specs=[anywhere] * (3 + levels),
         scratch_shapes=[
             pltpu.VMEM((2 * levels * BLOCK, width), jnp.bfloat16),
             pltpu.VMEM((2, 2, BLOCK, HALF_Q), jnp.bfloat16),
@@ -232,7 +233,7 @@
         + [pltpu.VMEM(term.shape, term.dtype) for term in terms]
         + [
             pltpu.SemaphoreType.DMA((HALF_KV, levels + 4)),
-            pltpu.SemaphoreType.DMA((HALF_KV * (levels + 2),)),
+            pltpu.SemaphoreType.DMA((HALF_KV * (levels + 3),)),
         ],
         compiler_params=pltpu.CompilerParams(vmem_limit_bytes=60 * 1024 * 1024),
         cost_estimate=pl.CostEstimate(
@@ -287,7 +288,7 @@
         held.append(lax.ppermute(held[0], "blk", pairs))
 
     top = levels - 1
-    own_out, partner_out, here, near, *between, first = attention(
+    own_out, partner_out, here, near, *between, first, second = attention(
         levels,
         block_lists[0, 0],
         list_counts[0],
@@ -300,22 +301,28 @@
         held,
     )
 
-    def down(terms, hop, lowest):
-        pairs = [(i, i - 2 * hop) for i in range(2 * lowest, blocks)]
+    def down(terms, hop, levels_from):
+        pairs = [(2 * z + p, 2 * (z - hop) + p) for z in levels_from for p in range(2)]
         return lax.ppermute(terms, "blk", pairs)
 
-    landed = down(first, 1, 1)
+    landed = down(first, 1, range(1, levels))
     query_grads = (back(own_out, lambda b: b), back(partner_out, lambda b: b ^ 1))
+    skipped = down(second, 2, [top])
     carried = landed
     for j in range(top - 1, 1, -1):
         total = between[j - 2] + carried.astype(jnp.float32)
         total = total.astype(jnp.bfloat16)
-        carried = down(total, 1, j) if j > 2 else down(total, 2, 2)
+        if j == 2:
+            near, total = lax.optimization_barrier((near, total))
+        carried = down(total, 1, range(j, levels)) if j > 2 else down(total, 2, range(2, top))
+    rest = down(near, 1, [top])
     here = here + jnp.where(level == top - 1, 0.0, landed.astype(jnp.float32))
-    near, here = lax.optimization_barrier((near, here))
-    rest = down(near, 1, top)
-    rest, query_grads, carried = lax.optimization_barrier((rest, query_grads, carried))
-    totals = (here + carried.astype(jnp.float32) + rest.astype(jnp.float32)).astype(jnp.bfloat16)
+    rest, skipped, query_grads, carried = lax.optimization_barrier(
+        (rest, skipped, query_grads, carried)
+    )
+    for terms in (carried, skipped, rest):
+        here = here + terms.astype(jnp.float32)
+    totals = here.astype(jnp.bfloat16)
     sums = [back(totals[:BLOCK], lambda b: b), back(totals[BLOCK:], lambda b: b ^ 1)]
 
     def ordered(a, b):

time: 76.9 us -> 76.3 us (level); the launches traced: 75.6 us -> 75.9 us
  waiting for transfers between devices: 28.5 us -> 32.7 us
  starting transfers between devices: 25.7 us -> 22 us
    ppermute x3 -> x4, waiting for transfers between devices: 11 us -> 15.7 us  [down(): return lax.ppermute(terms, 'blk', pairs)]
    ppermute x4, starting transfers between devices: 10.2 us -> 5.66 us  [back(): return lax.ppermute(value, ('section', 'blk'), pairs)]
    ppermute x3 -> x4, starting transfers between devices: 3.26 us -> 4.06 us  [down(): return lax.ppermute(terms, 'blk', pairs)]
  transfers between devices with their start and end apart: 13 -> 14, of which waited for: 6 -> 6; matrix products, arithmetic and copies ran while one was open for 6% -> 6% of each run, Pallas kernels for 0% -> 0%
where the time goes in v4:
time: 76.3 us; the launch traced here: 75.9 us
  waiting for transfers between devices  32.7 us (43%)
  starting transfers between devices  22 us (29%)
  Pallas kernels  11.5 us (15%)
  other arithmetic  4.72 us (6%)
  local copies, waits for them, and re-layouts  3.46 us (5%)
  between operations  1.59 us (2%)
    ppermute x4, waiting for transfers between devices, down(): return lax.ppermute(terms, 'blk', pairs)  15.7 us
    ppermute x1, waiting for transfers between devices, per_device(): told = lax.ppermute(facts, 'blk', swap)  11.9 us
    pallas_call x1, Pallas kernels, attention(): pl.pallas_call(lambda *refs: attention_kernel(levels, *refs), out_shape=o...  11.5 us
    ppermute x3, starting transfers between devices, per_device(): held.append(lax.ppermute(held[0], 'blk', pairs))  8.74 us
    ppermute x4, starting transfers between devices, back(): return lax.ppermute(value, ('section', 'blk'), pairs)  5.66 us
    ppermute x4, starting transfers between devices, down(): return lax.ppermute(terms, 'blk', pairs)  4.06 us
    ppermute x4, waiting for transfers between devices, back(): return lax.ppermute(value, ('section', 'blk'), pairs)  3.33 us
    select_n x3, other arithmetic, ordered(): jnp.where(side == 0, jnp.concatenate([a, b], axis=1), jnp.concatenate([b,...  2.59 us
  transfers between devices with their start and end apart: 14, of which 6 were waited for; matrix products, arithmetic and copies ran while one was open for 6% of the time, Pallas kernels for 0%

profile of v4, /device:TPU:1, one launch (start us, length us, event | category | flops | bytes accessed | tf_op | source)
XLA Modules:
  0.0 75.9 jit_solution(6854901782633198636)
XLA Ops:
  0.7 0.9 %dynamic-slice_bitcast_fusion.4 = (bf16[128,128]{1,0:T(8,128)(2,1)S(1)}, bf16[128,128]{1,0:T(8,128)(2,1)S(1)}, bf16[128,128]{1,0:T(8,128)(2,1)S(1)}, bf16[128,12...) fusion(bf16[1,128,512]{2,1,0:T(8,128)(2,1)} %param.9, ...), kind=kLoop, calls=%fused_computation.26 | loop fusion | bytes 524304 | tf_op jit(solution)/shard_map/dynamic_slice | solution.py:268
  1.6 2.1 %collective-permute-start.1 = (bf16[128,512]{1,0:T(8,128)(2,1)S(1)}, bf16[128,512]{1,0:T(8,128)(2,1)S(1)}, u32[]{:S(2)}, u32[]{:S(2)}) collective-permute-start(bf16[128,512]{1,0:T(8,128)(2,1)S(1)} %pad_maximum_fusion.2), channel_id=1, source_target_pairs={{0,1},{1,0},{2,3},{3,2},{4,5},{5,4},{6,7},{7,6},{8,9},{9,8},{10,11... | collective-permute-start | bytes 393224 | tf_op jit(solution)/shard_map/ppermute | solution.py:279
  3.7 1.3 %dynamic-slice_bitcast_fusion = (bf16[128,2048]{1,0:T(8,128)(2,1)S(1)}, bf16[128,2048]{1,0:T(8,128)(2,1)S(1)}) fusion(bf16[1,128,4096]{2,1,0:T(8,128)(2,1)} %param.10, s32[]{:T(128)S(6)} %select_n.88, bf16[1,128,4096]{2,1,0:T(8,128)(2,1)} %param.7), kind=kLoop, calls=%fused_computation.10 | loop fusion | bytes 2097156 | tf_op jit(solution)/shard_map/dynamic_slice | solution.py:268
  5.1 1.8 %collective-permute-done.1 = bf16[128,512]{1,0:T(8,128)(2,1)S(1)} collective-permute-done((bf16[128,512]{1,0:T(8,128)(2,1)S(1)}, bf16[128,512]{1,0:T(8,128)(2,1)S(1)}, u32[]{:S(2)}, u32[]{:S(2)}) %collective-permute-start.1) | collective-permute-done | bytes 131104 | tf_op jit(solution)/shard_map/ppermute | solution.py:279
  7.0 1.1 %collective-permute-start.2 = (bf16[128,4096]{1,0:T(8,128)(2,1)S(1)}, bf16[128,4096]{1,0:T(8,128)(2,1)S(1)}, u32[]{:S(2)}, u32[]{:S(2)}) collective-permute-start(bf16[128,4096]{1,0:T(8,128)(2,1)S(1)} %pad_maximum_fusion), channel_id=1, source_target_pairs={{0,1},{1,0},{2,3},{3,2},{4,5},{5,4},{6,7},{7,6},{8,9},{9,8},{10,11... | collective-permute-start | bytes 3145736 | tf_op jit(solution)/shard_map/ppermute | solution.py:284
  8.1 3.2 %collective-permute-start.5 = (bf16[256,512]{1,0:T(8,128)(2,1)S(1)}, bf16[256,512]{1,0:T(8,128)(2,1)S(1)}, u32[]{:S(2)}, u32[]{:S(2)}) collective-permute-start(bf16[256,512]{1,0:T(8,128)(2,1)S(1)} %pad_maximum_fusion.1.refs_11_), channel_id=1, source_target_pairs={{0,2},{1,3},{2,4},{3,5},{4,6},{5,7},{8,10},{9,11},{10,12},{11,13},... | collective-permute-start | bytes 786440 | tf_op jit(solution)/shard_map/ppermute | solution.py:288
  11.4 4.2 %collective-permute-start.4 = (bf16[256,512]{1,0:T(8,128)(2,1)S(1)}, bf16[256,512]{1,0:T(8,128)(2,1)S(1)}, u32[]{:S(2)}, u32[]{:S(2)}) collective-permute-start(bf16[256,512]{1,0:T(8,128)(2,1)S(1)} %pad_maximum_fusion.1.refs_11_), channel_id=1, source_target_pairs={{0,4},{1,5},{2,6},{3,7},{8,12},{9,13},{10,14},{11,15},{16,20},{17,... | collective-permute-start | bytes 786440 | tf_op jit(solution)/shard_map/ppermute | solution.py:288
  15.6 1.3 %collective-permute-start.3 = (bf16[256,512]{1,0:T(8,128)(2,1)S(1)}, bf16[256,512]{1,0:T(8,128)(2,1)S(1)}, u32[]{:S(2)}, u32[]{:S(2)}) collective-permute-start(bf16[256,512]{1,0:T(8,128)(2,1)S(1)} %pad_maximum_fusion.1.refs_11_), channel_id=1, source_target_pairs={{0,6},{1,7},{8,14},{9,15},{16,22},{17,23},{24,30},{25,31}} | collective-permute-start | bytes 786440 | tf_op jit(solution)/shard_map/ppermute | solution.py:288
  17.6 0.2 collective-permute-start
  17.9 0.7 pad_add_fusion.1.refs_2_
  18.5 11.9 %collective-permute-done.refs_4_ = s32[1,133]{1,0:T(1,128)S(1)} collective-permute-done((s32[1,133]{1,0:T(1,128)S(1)}, s32[1,133]{1,0:T(1,128)S(1)}, u32[]{:S(2)}, u32[]{:S(2)}) %collective-permute-start) | collective-permute-done | bytes 564 | tf_op jit(solution)/shard_map/ppermute | solution.py:278
  30.5 0.5 copy-done.9
  31.0 0.2 copy-done.5
  31.3 0.4 copy-done.4
  31.6 11.5 %shard_map.94 = (bf16[128,2048]{1,0:T(8,128)(2,1)}, bf16[128,2048]{1,0:T(8,128)(2,1)}, f32[256,512]{1,0:T(8,128)}, bf16[256,512]{1,0:T(8,128)(2,1)}, f32[256,512...) custom-call(s32[4]{0:T(128)} %bitcast.53, s32[1]{0:T(128)} %bitcast.47.refs_1_, ...), custom_call_target="tpu_custom_call" | custom-call | flops 2684354560 | bytes 8388608 | tf_op jit(solution)/shard_map/pallas_call | solution.py:216
  43.1 1.4 %collective-permute-start.6 = (bf16[256,512]{1,0:T(8,128)(2,1)}, bf16[256,512]{1,0:T(8,128)(2,1)S(1)}, u32[]{:S(2)}, u32[]{:S(2)}) collective-permute-start(bf16[256,512]{1,0:T(8,128)(2,1)} %get-tuple-element.23), channel_id=1, source_target_pairs={{2,0},{3,1},{4,2},{5,3},{6,4},{7,5},{10,8},{11,9},{12,10},{13,11},... | collective-permute-start | bytes 786440 | tf_op jit(solution)/shard_map/ppermute | solution.py:306
  44.6 2.2 %collective-permute-start.9 = (bf16[128,2048]{1,0:T(8,128)(2,1)}, bf16[128,2048]{1,0:T(8,128)(2,1)S(1)}, u32[]{:S(2)}, u32[]{:S(2)}) collective-permute-start(bf16[128,2048]{1,0:T(8,128)(2,1)} %get-tuple-element.26), channel_id=1, source_target_pairs={{0,24},{1,25},{2,26},{3,27},{4,28},{5,29},{6,30},{7,31},{8,0},{9,1... | collective-permute-start | bytes 1572872 | tf_op jit(solution)/shard_map/ppermute | solution.py:265
  46.8 1.1 %collective-permute-start.10 = (bf16[128,2048]{1,0:T(8,128)(2,1)}, bf16[128,2048]{1,0:T(8,128)(2,1)S(1)}, u32[]{:S(2)}, u32[]{:S(2)}) collective-permute-start(bf16[128,2048]{1,0:T(8,128)(2,1)} %get-tuple-element.27), channel_id=1, source_target_pairs={{0,25},{1,24},{2,27},{3,26},{4,29},{5,28},{6,31},{7,30},{8,1},{9,0... | collective-permute-start | bytes 1572872 | tf_op jit(solution)/shard_map/ppermute | solution.py:265
  47.9 0.7 collective-permute-start.8
  48.6 3.6 %collective-permute-done.6 = bf16[256,512]{1,0:T(8,128)(2,1)S(1)} collective-permute-done((bf16[256,512]{1,0:T(8,128)(2,1)}, bf16[256,512]{1,0:T(8,128)(2,1)S(1)}, u32[]{:S(2)}, u32[]{:S(2)}) %collective-permute-start.6) | collective-permute-done | bytes 262176 | tf_op jit(solution)/shard_map/ppermute | solution.py:306
  52.2 1.1 %fusion = bf16[256,512]{1,0:T(8,128)(2,1)S(1)} fusion(f32[256,512]{1,0:T(8,128)} %get-tuple-element.22, bf16[256,512]{1,0:T(8,128)(2,1)S(1)} %collective-permute-done.6), kind=kLoop, calls=%fused_computation.4 | loop fusion | flops 393216 | bytes 1048576 | tf_op jit(solution)/shard_map/convert_element_type | solution.py:314
  53.3 0.7 collective-permute-start.7
  54.0 1.3 %collective-permute-start.11 = (bf16[256,512]{1,0:T(8,128)(2,1)S(1)}, bf16[256,512]{1,0:T(8,128)(2,1)S(1)}, u32[]{:S(2)}, u32[]{:S(2)}) collective-permute-start(bf16[256,512]{1,0:T(8,128)(2,1)S(1)} %fusion), channel_id=1, source_target_pairs={{4,0},{5,1},{12,8},{13,9},{20,16},{21,17},{28,24},{29,25}} | collective-permute-start | bytes 786440 | tf_op jit(solution)/shard_map/ppermute | solution.py:306
  55.3 12.1 %collective-permute-done.11 = bf16[256,512]{1,0:T(8,128)(2,1)S(1)} collective-permute-done((bf16[256,512]{1,0:T(8,128)(2,1)S(1)}, bf16[256,512]{1,0:T(8,128)(2,1)S(1)}, u32[]{:S(2)}, u32[]{:S(2)}) %collective-permute-start.11) | collective-permute-done | bytes 262176 | tf_op jit(solution)/shard_map/ppermute | solution.py:306
  67.4 0.2 fusion.5
  67.6 1.6 %collective-permute-start.12 = (bf16[128,512]{1,0:T(8,128)(2,1)S(1)}, bf16[128,512]{1,0:T(8,128)(2,1)S(1)}, u32[]{:S(2)}, u32[]{:S(2)}) collective-permute-start(bf16[128,512]{1,0:T(8,128)(2,1)S(1)} %get-tuple-element.35), channel_id=1, source_target_pairs={{0,24},{1,25},{2,26},{3,27},{4,28},{5,29},{6,30},{7,31},{8,0},{9,1... | collective-permute-start | bytes 393224 | tf_op jit(solution)/shard_map/ppermute | solution.py:265
  69.2 0.7 collective-permute-start.13
  69.9 1.2 %maximum_select_fusion = bf16[1,128,4096]{2,1,0:T(8,128)(2,1)} fusion(bf16[1,128,2048]{2,1,0:T(8,128)(2,1)S(1)} %bitcast.49, bf16[1,128,2048]{2,1,0:T(8,128)(2,1)S(1)} %bitcast.48, pred[]{:T(512)S(6)} %eq.13), kind=kLoop, calls=%fused_computation.1 | loop fusion | flops 4718592 | bytes 2097153 | tf_op jit(solution)/shard_map/jit(_where)/select_n | solution.py:329
  71.1 2.1 %collective-permute-done.12 = bf16[128,512]{1,0:T(8,128)(2,1)S(1)} collective-permute-done((bf16[128,512]{1,0:T(8,128)(2,1)S(1)}, bf16[128,512]{1,0:T(8,128)(2,1)S(1)}, u32[]{:S(2)}, u32[]{:S(2)}) %collective-permute-start.12) | collective-permute-done | bytes 131104 | tf_op jit(solution)/shard_map/ppermute | solution.py:265
  73.3 1.2 %collective-permute-done.13 = bf16[128,512]{1,0:T(8,128)(2,1)S(1)} collective-permute-done((bf16[128,512]{1,0:T(8,128)(2,1)S(1)}, bf16[128,512]{1,0:T(8,128)(2,1)S(1)}, u32[]{:S(2)}, u32[]{:S(2)}) %collective-permute-start.13) | collective-permute-done | bytes 131104 | tf_op jit(solution)/shard_map/ppermute | solution.py:265
  74.5 0.7 maximum_select_fusion.2
  75.2 0.7 maximum_select_fusion.1
  (32 shorter events, 0.5 us)
Async XLA Ops:
  1.6 5.4 %collective-permute-start.1 = (bf16[128,512]{1,0:T(8,128)(2,1)S(1)}, bf16[128,512]{1,0:T(8,128)(2,1)S(1)}, u32[]{:S(2)}, u32[]{:S(2)}) collective-permute-start(bf16[128,512]{1,0:T(8,128)(2,1)S(1)} %pad_maximum_fusion.2), channel_id=1, source_target_pairs={{0,1},{1,0},{2,3},{3,2},{4,5},{5,4},{6,7},{7,6},{8,9},{9,8},{10,11... | collective-permute-start | bytes 393224 | tf_op jit(solution)/shard_map/ppermute | solution.py:279
  5.0 12.5 %copy-start.2 = (s32[1,1,4]{2,1,0:T(1,128)S(1)}, s32[1,1,4]{2,1,0:T(1,128)}, u32[]{:S(2)}) copy-start(s32[1,1,4]{2,1,0:T(1,128)} %param.12) | copy-start | bytes 52
  5.1 12.5 %copy-start.3 = (s32[1,128]{1,0:T(1,128)S(1)}, s32[1,128]{1,0:T(1,128)}, u32[]{:S(2)}) copy-start(s32[1,128]{1,0:T(1,128)} %refs_3_.1) | copy-start | bytes 1540
  7.0 23.5 %collective-permute-start.2 = (bf16[128,4096]{1,0:T(8,128)(2,1)S(1)}, bf16[128,4096]{1,0:T(8,128)(2,1)S(1)}, u32[]{:S(2)}, u32[]{:S(2)}) collective-permute-start(bf16[128,4096]{1,0:T(8,128)(2,1)S(1)} %pad_maximum_fusion), channel_id=1, source_target_pairs={{0,1},{1,0},{2,3},{3,2},{4,5},{5,4},{6,7},{7,6},{8,9},{9,8},{10,11... | collective-permute-start | bytes 3145736 | tf_op jit(solution)/shard_map/ppermute | solution.py:284
  8.1 22.3 %copy-start.1 = (bf16[256,512]{1,0:T(8,128)(2,1)}, bf16[256,512]{1,0:T(8,128)(2,1)S(1)}, u32[]{:S(2)}) copy-start(bf16[256,512]{1,0:T(8,128)(2,1)S(1)} %pad_maximum_fusion.1.refs_11_) | copy-start | bytes 786436
  8.1 22.3 %collective-permute-start.5 = (bf16[256,512]{1,0:T(8,128)(2,1)S(1)}, bf16[256,512]{1,0:T(8,128)(2,1)S(1)}, u32[]{:S(2)}, u32[]{:S(2)}) collective-permute-start(bf16[256,512]{1,0:T(8,128)(2,1)S(1)} %pad_maximum_fusion.1.refs_11_), channel_id=1, source_target_pairs={{0,2},{1,3},{2,4},{3,5},{4,6},{5,7},{8,10},{9,11},{10,12},{11,13},... | collective-permute-start | bytes 786440 | tf_op jit(solution)/shard_map/ppermute | solution.py:288
  11.4 19.0 %collective-permute-start.4 = (bf16[256,512]{1,0:T(8,128)(2,1)S(1)}, bf16[256,512]{1,0:T(8,128)(2,1)S(1)}, u32[]{:S(2)}, u32[]{:S(2)}) collective-permute-start(bf16[256,512]{1,0:T(8,128)(2,1)S(1)} %pad_maximum_fusion.1.refs_11_), channel_id=1, source_target_pairs={{0,4},{1,5},{2,6},{3,7},{8,12},{9,13},{10,14},{11,15},{16,20},{17,... | collective-permute-start | bytes 786440 | tf_op jit(solution)/shard_map/ppermute | solution.py:288
  15.6 14.8 %collective-permute-start.3 = (bf16[256,512]{1,0:T(8,128)(2,1)S(1)}, bf16[256,512]{1,0:T(8,128)(2,1)S(1)}, u32[]{:S(2)}, u32[]{:S(2)}) collective-permute-start(bf16[256,512]{1,0:T(8,128)(2,1)S(1)} %pad_maximum_fusion.1.refs_11_), channel_id=1, source_target_pairs={{0,6},{1,7},{8,14},{9,15},{16,22},{17,23},{24,30},{25,31}} | collective-permute-start | bytes 786440 | tf_op jit(solution)/shard_map/ppermute | solution.py:288
  17.6 12.8 %collective-permute-start = (s32[1,133]{1,0:T(1,128)S(1)}, s32[1,133]{1,0:T(1,128)S(1)}, u32[]{:S(2)}, u32[]{:S(2)}) collective-permute-start(s32[1,133]{1,0:T(1,128)S(1)} %bitcast.52), channel_id=1, source_target_pairs={{0,1},{1,0},{2,3},{3,2},{4,5},{5,4},{6,7},{7,6},{8,9},{9,8},{10,11... | collective-permute-start | bytes 1604 | tf_op jit(solution)/shard_map/ppermute | solution.py:278
  30.4 0.6 copy-start.9
  30.4 0.7 copy-start.5
  30.4 0.8 %copy-start.6 = (bf16[256,512]{1,0:T(8,128)(2,1)}, bf16[256,512]{1,0:T(8,128)(2,1)S(1)}, u32[]{:S(2)}) copy-start(bf16[256,512]{1,0:T(8,128)(2,1)S(1)} %collective-permute-done.4.refs_9_) | copy-start | bytes 786436
  30.4 0.8 %copy-start.7 = (bf16[256,512]{1,0:T(8,128)(2,1)}, bf16[256,512]{1,0:T(8,128)(2,1)S(1)}, u32[]{:S(2)}) copy-start(bf16[256,512]{1,0:T(8,128)(2,1)S(1)} %collective-permute-done.3.refs_8_) | copy-start | bytes 786436
  30.5 1.2 %copy-start.4 = (bf16[128,4096]{1,0:T(8,128)(2,1)}, bf16[128,4096]{1,0:T(8,128)(2,1)S(1)}, u32[]{:S(2)}) copy-start(bf16[128,4096]{1,0:T(8,128)(2,1)S(1)} %collective-permute-done.2.refs_7_) | copy-start | bytes 3145732
  43.1 10.2 %copy-start.8 = (bf16[256,512]{1,0:T(8,128)(2,1)S(1)}, bf16[256,512]{1,0:T(8,128)(2,1)}, u32[]{:S(2)}) copy-start(bf16[256,512]{1,0:T(8,128)(2,1)} %get-tuple-element.24) | copy-start | bytes 786436
  43.1 24.3 %copy-start = (f32[256,512]{1,0:T(8,128)S(1)}, f32[256,512]{1,0:T(8,128)}, u32[]{:S(2)}) copy-start(f32[256,512]{1,0:T(8,128)} %get-tuple-element.31) | copy-start | bytes 1572868
  43.1 9.1 %collective-permute-start.6 = (bf16[256,512]{1,0:T(8,128)(2,1)}, bf16[256,512]{1,0:T(8,128)(2,1)S(1)}, u32[]{:S(2)}, u32[]{:S(2)}) collective-permute-start(bf16[256,512]{1,0:T(8,128)(2,1)} %get-tuple-element.23), channel_id=1, source_target_pairs={{2,0},{3,1},{4,2},{5,3},{6,4},{7,5},{10,8},{11,9},{12,10},{13,11},... | collective-permute-start | bytes 786440 | tf_op jit(solution)/shard_map/ppermute | solution.py:306
  44.6 22.8 %collective-permute-start.9 = (bf16[128,2048]{1,0:T(8,128)(2,1)}, bf16[128,2048]{1,0:T(8,128)(2,1)S(1)}, u32[]{:S(2)}, u32[]{:S(2)}) collective-permute-start(bf16[128,2048]{1,0:T(8,128)(2,1)} %get-tuple-element.26), channel_id=1, source_target_pairs={{0,24},{1,25},{2,26},{3,27},{4,28},{5,29},{6,30},{7,31},{8,0},{9,1... | collective-permute-start | bytes 1572872 | tf_op jit(solution)/shard_map/ppermute | solution.py:265
  46.8 20.6 %collective-permute-start.10 = (bf16[128,2048]{1,0:T(8,128)(2,1)}, bf16[128,2048]{1,0:T(8,128)(2,1)S(1)}, u32[]{:S(2)}, u32[]{:S(2)}) collective-permute-start(bf16[128,2048]{1,0:T(8,128)(2,1)} %get-tuple-element.27), channel_id=1, source_target_pairs={{0,25},{1,24},{2,27},{3,26},{4,29},{5,28},{6,31},{7,30},{8,1},{9,0... | collective-permute-start | bytes 1572872 | tf_op jit(solution)/shard_map/ppermute | solution.py:265
  47.9 7.4 %collective-permute-start.8 = (bf16[256,512]{1,0:T(8,128)(2,1)}, bf16[256,512]{1,0:T(8,128)(2,1)S(1)}, u32[]{:S(2)}, u32[]{:S(2)}) collective-permute-start(bf16[256,512]{1,0:T(8,128)(2,1)} %get-tuple-element.25), channel_id=1, source_target_pairs={{6,2},{7,3},{14,10},{15,11},{22,18},{23,19},{30,26},{31,27}} | collective-permute-start | bytes 786440 | tf_op jit(solution)/shard_map/ppermute | solution.py:306
  53.3 2.0 %collective-permute-start.7 = (bf16[256,512]{1,0:T(8,128)(2,1)S(1)}, bf16[256,512]{1,0:T(8,128)(2,1)S(1)}, u32[]{:S(2)}, u32[]{:S(2)}) collective-permute-start(bf16[256,512]{1,0:T(8,128)(2,1)S(1)} %copy-done.8), channel_id=1, source_target_pairs={{6,4},{7,5},{14,12},{15,13},{22,20},{23,21},{30,28},{31,29}} | collective-permute-start | bytes 786440 | tf_op jit(solution)/shard_map/ppermute | solution.py:306
  54.0 13.4 %collective-permute-start.11 = (bf16[256,512]{1,0:T(8,128)(2,1)S(1)}, bf16[256,512]{1,0:T(8,128)(2,1)S(1)}, u32[]{:S(2)}, u32[]{:S(2)}) collective-permute-start(bf16[256,512]{1,0:T(8,128)(2,1)S(1)} %fusion), channel_id=1, source_target_pairs={{4,0},{5,1},{12,8},{13,9},{20,16},{21,17},{28,24},{29,25}} | collective-permute-start | bytes 786440 | tf_op jit(solution)/shard_map/ppermute | solution.py:306
  67.6 5.6 %collective-permute-start.12 = (bf16[128,512]{1,0:T(8,128)(2,1)S(1)}, bf16[128,512]{1,0:T(8,128)(2,1)S(1)}, u32[]{:S(2)}, u32[]{:S(2)}) collective-permute-start(bf16[128,512]{1,0:T(8,128)(2,1)S(1)} %get-tuple-element.35), channel_id=1, source_target_pairs={{0,24},{1,25},{2,26},{3,27},{4,28},{5,29},{6,30},{7,31},{8,0},{9,1... | collective-permute-start | bytes 393224 | tf_op jit(solution)/shard_map/ppermute | solution.py:265
  69.2 5.3 %collective-permute-start.13 = (bf16[128,512]{1,0:T(8,128)(2,1)S(1)}, bf16[128,512]{1,0:T(8,128)(2,1)S(1)}, u32[]{:S(2)}, u32[]{:S(2)}) collective-permute-start(bf16[128,512]{1,0:T(8,128)(2,1)S(1)} %get-tuple-element.36), channel_id=1, source_target_pairs={{0,25},{1,24},{2,27},{3,26},{4,29},{5,28},{6,31},{7,30},{8,1},{9,0... | collective-permute-start | bytes 393224 | tf_op jit(solution)/shard_map/ppermute | solution.py:265

commit v5 on v4

--- a/solution.py
+++ b/solution.py
@@ -36,13 +36,12 @@
     query_ref, grad_ref, partner_ref = refs[4:7]
     held = refs[7 : 7 + levels][::-1]
     outs = refs[7 + levels : 9 + levels]
-    term_refs = refs[9 + levels : 10 + 2 * levels]
-    scratch = refs[10 + 2 * levels :]
+    term_refs = refs[9 + levels : 9 + 2 * levels]
+    scratch = refs[9 + 2 * levels :]
     rows_of = [pl.ds(2 * j * BLOCK, 2 * BLOCK) for j in range(levels - 1)]
     rows_of.append(pl.ds(pl.multiple_of(2 * where_ref[1] * BLOCK, 2 * BLOCK), 2 * BLOCK))
-    rows_of.append(rows_of[2])
     kv, rows_in, rows_out, bias, probs, dscores, sums = scratch[:7]
-    terms = scratch[7 : 8 + levels]
+    terms = scratch[7 : 7 + levels]
     arrived, left = scratch[-2:]
 
     mine = where_ref[0]
@@ -193,7 +192,7 @@
                 sums[places[block][slot], key_cols] += key_terms[at]
                 sums[places[block][slot], value_cols] += value_terms[at]
         cols = slice(group * PAIR, (group + 1) * PAIR)
-        for j in range(levels + 1):
+        for j in range(levels):
             terms[j][:, cols] = sums[rows_of[j], cols].astype(terms[j].dtype)
             cut = pl.ds(group * PAIR, PAIR)
             send(terms[j].at[:, cut], term_refs[j].at[:, cut])
@@ -209,9 +208,9 @@
     outs = [jax.ShapeDtypeStruct((BLOCK, HALF_Q), jnp.bfloat16)] * 2
     terms = [
         jax.ShapeDtypeStruct(
-            (2 * BLOCK, width), jnp.bfloat16 if j in (1, levels - 1, levels) else jnp.float32
+            (2 * BLOCK, width), jnp.float32 if j == 0 else jnp.bfloat16
         )
-        for j in range(levels + 1)
+        for j in range(levels)
     ]
     return pl.pallas_call(
         lambda *refs: attention_kernel(levels, *refs),
@@ -220,7 +219,7 @@
             pl.BlockSpec(memory_space=pltpu.VMEM)
         ]
         + [anywhere] * (3 + levels),
-        out_specs=[anywhere] * (3 + levels),
+        out_specs=[anywhere] * (2 + levels),
         scratch_shapes=[
             pltpu.VMEM((2 * levels * BLOCK, width), jnp.bfloat16),
             pltpu.VMEM((2, 2, BLOCK, HALF_Q), jnp.bfloat16),
@@ -233,7 +232,7 @@
         + [pltpu.VMEM(term.shape, term.dtype) for term in terms]
         + [
             pltpu.SemaphoreType.DMA((HALF_KV, levels + 4)),
-            pltpu.SemaphoreType.DMA((HALF_KV * (levels + 3),)),
+            pltpu.SemaphoreType.DMA((HALF_KV * (levels + 2),)),
         ],
         compiler_params=pltpu.CompilerParams(vmem_limit_bytes=60 * 1024 * 1024),
         cost_estimate=pl.CostEstimate(
@@ -288,7 +287,7 @@
         held.append(lax.ppermute(held[0], "blk", pairs))
 
     top = levels - 1
-    own_out, partner_out, here, near, *between, first, second = attention(
+    own_out, partner_out, here, near, *between, first = attention(
         levels,
         block_lists[0, 0],
         list_counts[0],
@@ -307,10 +306,10 @@
 
     landed = down(first, 1, range(1, levels))
     query_grads = (back(own_out, lambda b: b), back(partner_out, lambda b: b ^ 1))
-    skipped = down(second, 2, [top])
+    skipped = down(between[0], 2, [top])
     carried = landed
     for j in range(top - 1, 1, -1):
-        total = between[j - 2] + carried.astype(jnp.float32)
+        total = between[j - 2].astype(jnp.float32) + carried.astype(jnp.float32)
         total = total.astype(jnp.bfloat16)
         if j == 2:
             near, total = lax.optimization_barrier((near, total))

time: 76.3 us -> 76.1 us (level)
  no operation moved by 1% of the time
where the time goes in v5:
time: 76.1 us; the launch traced here: 75.7 us
  waiting for transfers between devices  33 us (43%)
  starting transfers between devices  21.9 us (29%)
  Pallas kernels  11.3 us (15%)
  other arithmetic  4.53 us (6%)
  local copies, waits for them, and re-layouts  3.46 us (5%)
  between operations  1.57 us (2%)
    ppermute x4, waiting for transfers between devices, down(): return lax.ppermute(terms, 'blk', pairs)  15.9 us
    ppermute x1, waiting for transfers between devices, per_device(): told = lax.ppermute(facts, 'blk', swap)  12 us
    pallas_call x1, Pallas kernels, attention(): pl.pallas_call(lambda *refs: attention_kernel(levels, *refs), out_shape=o...  11.3 us
    ppermute x3, starting transfers between devices, per_device(): held.append(lax.ppermute(held[0], 'blk', pairs))  8.74 us
    ppermute x4, starting transfers between devices, back(): return lax.ppermute(value, ('section', 'blk'), pairs)  5.6 us
    ppermute x4, starting transfers between devices, down(): return lax.ppermute(terms, 'blk', pairs)  4.06 us
    ppermute x4, waiting for transfers between devices, back(): return lax.ppermute(value, ('section', 'blk'), pairs)  3.3 us
    select_n x3, other arithmetic, ordered(): jnp.where(side == 0, jnp.concatenate([a, b], axis=1), jnp.concatenate([b,...  2.59 us
  transfers between devices with their start and end apart: 14, of which 6 were waited for; matrix products, arithmetic and copies ran while one was open for 6% of the time, Pallas kernels for 0%

profile of v5, /device:TPU:1, one launch (start us, length us, event | category | flops | bytes accessed | tf_op | source)
XLA Modules:
  0.0 75.7 jit_solution(11337571474841768109)
XLA Ops:
  0.7 0.9 %dynamic-slice_bitcast_fusion.4 = (bf16[128,128]{1,0:T(8,128)(2,1)S(1)}, bf16[128,128]{1,0:T(8,128)(2,1)S(1)}, bf16[128,128]{1,0:T(8,128)(2,1)S(1)}, bf16[128,12...) fusion(bf16[1,128,512]{2,1,0:T(8,128)(2,1)} %param.9, ...), kind=kLoop, calls=%fused_computation.26 | loop fusion | bytes 524304 | tf_op jit(solution)/shard_map/dynamic_slice | solution.py:267
  1.6 2.1 %collective-permute-start.1 = (bf16[128,512]{1,0:T(8,128)(2,1)S(1)}, bf16[128,512]{1,0:T(8,128)(2,1)S(1)}, u32[]{:S(2)}, u32[]{:S(2)}) collective-permute-start(bf16[128,512]{1,0:T(8,128)(2,1)S(1)} %pad_maximum_fusion.2), channel_id=1, source_target_pairs={{0,1},{1,0},{2,3},{3,2},{4,5},{5,4},{6,7},{7,6},{8,9},{9,8},{10,11... | collective-permute-start | bytes 393224 | tf_op jit(solution)/shard_map/ppermute | solution.py:278
  3.7 1.3 %dynamic-slice_bitcast_fusion = (bf16[128,2048]{1,0:T(8,128)(2,1)S(1)}, bf16[128,2048]{1,0:T(8,128)(2,1)S(1)}) fusion(bf16[1,128,4096]{2,1,0:T(8,128)(2,1)} %param.10, s32[]{:T(128)S(6)} %select_n.88, bf16[1,128,4096]{2,1,0:T(8,128)(2,1)} %param.7), kind=kLoop, calls=%fused_computation.10 | loop fusion | bytes 2097156 | tf_op jit(solution)/shard_map/dynamic_slice | solution.py:267
  5.1 1.8 %collective-permute-done.1 = bf16[128,512]{1,0:T(8,128)(2,1)S(1)} collective-permute-done((bf16[128,512]{1,0:T(8,128)(2,1)S(1)}, bf16[128,512]{1,0:T(8,128)(2,1)S(1)}, u32[]{:S(2)}, u32[]{:S(2)}) %collective-permute-start.1) | collective-permute-done | bytes 131104 | tf_op jit(solution)/shard_map/ppermute | solution.py:278
  7.0 1.1 %collective-permute-start.2 = (bf16[128,4096]{1,0:T(8,128)(2,1)S(1)}, bf16[128,4096]{1,0:T(8,128)(2,1)S(1)}, u32[]{:S(2)}, u32[]{:S(2)}) collective-permute-start(bf16[128,4096]{1,0:T(8,128)(2,1)S(1)} %pad_maximum_fusion), channel_id=1, source_target_pairs={{0,1},{1,0},{2,3},{3,2},{4,5},{5,4},{6,7},{7,6},{8,9},{9,8},{10,11... | collective-permute-start | bytes 3145736 | tf_op jit(solution)/shard_map/ppermute | solution.py:283
  8.1 3.2 %collective-permute-start.5 = (bf16[256,512]{1,0:T(8,128)(2,1)S(1)}, bf16[256,512]{1,0:T(8,128)(2,1)S(1)}, u32[]{:S(2)}, u32[]{:S(2)}) collective-permute-start(bf16[256,512]{1,0:T(8,128)(2,1)S(1)} %pad_maximum_fusion.1.refs_11_), channel_id=1, source_target_pairs={{0,2},{1,3},{2,4},{3,5},{4,6},{5,7},{8,10},{9,11},{10,12},{11,13},... | collective-permute-start | bytes 786440 | tf_op jit(solution)/shard_map/ppermute | solution.py:287
  11.4 4.2 %collective-permute-start.4 = (bf16[256,512]{1,0:T(8,128)(2,1)S(1)}, bf16[256,512]{1,0:T(8,128)(2,1)S(1)}, u32[]{:S(2)}, u32[]{:S(2)}) collective-permute-start(bf16[256,512]{1,0:T(8,128)(2,1)S(1)} %pad_maximum_fusion.1.refs_11_), channel_id=1, source_target_pairs={{0,4},{1,5},{2,6},{3,7},{8,12},{9,13},{10,14},{11,15},{16,20},{17,... | collective-permute-start | bytes 786440 | tf_op jit(solution)/shard_map/ppermute | solution.py:287
  15.6 1.3 %collective-permute-start.3 = (bf16[256,512]{1,0:T(8,128)(2,1)S(1)}, bf16[256,512]{1,0:T(8,128)(2,1)S(1)}, u32[]{:S(2)}, u32[]{:S(2)}) collective-permute-start(bf16[256,512]{1,0:T(8,128)(2,1)S(1)} %pad_maximum_fusion.1.refs_11_), channel_id=1, source_target_pairs={{0,6},{1,7},{8,14},{9,15},{16,22},{17,23},{24,30},{25,31}} | collective-permute-start | bytes 786440 | tf_op jit(solution)/shard_map/ppermute | solution.py:287
  17.6 0.2 collective-permute-start
  17.9 0.6 pad_add_fusion.1.refs_2_
  18.4 12.0 %collective-permute-done.refs_4_ = s32[1,133]{1,0:T(1,128)S(1)} collective-permute-done((s32[1,133]{1,0:T(1,128)S(1)}, s32[1,133]{1,0:T(1,128)S(1)}, u32[]{:S(2)}, u32[]{:S(2)}) %collective-permute-start) | collective-permute-done | bytes 564 | tf_op jit(solution)/shard_map/ppermute | solution.py:277
  30.5 0.5 copy-done.8
  31.0 0.1 copy-done.5
  31.3 0.3 copy-done.4
  31.6 11.3 %shard_map.94 = (bf16[128,2048]{1,0:T(8,128)(2,1)}, bf16[128,2048]{1,0:T(8,128)(2,1)}, f32[256,512]{1,0:T(8,128)}, bf16[256,512]{1,0:T(8,128)(2,1)}, bf16[256,512]{1,0:T(8,128)(2,1)}, /*index=5*/bf16[256,512]{1,0:T(8,128)(2,1)}) custom-call(s32[4]{0:T(128)} %bitcast.53, s32[1]{0:T(128)} %bitcast.47.refs_1_, s32[2]{0:T(128)} %pad_add_fusion.1.refs_2_, ...), custom_call_target="tpu_custom_call" | custom-call | flops 2684354560 | bytes 8388608 | tf_op jit(solution)/shard_map/pallas_call | solution.py:215
  42.9 1.4 %collective-permute-start.6 = (bf16[256,512]{1,0:T(8,128)(2,1)}, bf16[256,512]{1,0:T(8,128)(2,1)S(1)}, u32[]{:S(2)}, u32[]{:S(2)}) collective-permute-start(bf16[256,512]{1,0:T(8,128)(2,1)} %get-tuple-element.22), channel_id=1, source_target_pairs={{2,0},{3,1},{4,2},{5,3},{6,4},{7,5},{10,8},{11,9},{12,10},{13,11},... | collective-permute-start | bytes 786440 | tf_op jit(solution)/shard_map/ppermute | solution.py:305
  44.4 2.2 %collective-permute-start.9 = (bf16[128,2048]{1,0:T(8,128)(2,1)}, bf16[128,2048]{1,0:T(8,128)(2,1)S(1)}, u32[]{:S(2)}, u32[]{:S(2)}) collective-permute-start(bf16[128,2048]{1,0:T(8,128)(2,1)} %get-tuple-element.24), channel_id=1, source_target_pairs={{0,24},{1,25},{2,26},{3,27},{4,28},{5,29},{6,30},{7,31},{8,0},{9,1... | collective-permute-start | bytes 1572872 | tf_op jit(solution)/shard_map/ppermute | solution.py:264
  46.6 1.1 %collective-permute-start.10 = (bf16[128,2048]{1,0:T(8,128)(2,1)}, bf16[128,2048]{1,0:T(8,128)(2,1)S(1)}, u32[]{:S(2)}, u32[]{:S(2)}) collective-permute-start(bf16[128,2048]{1,0:T(8,128)(2,1)} %get-tuple-element.25), channel_id=1, source_target_pairs={{0,25},{1,24},{2,27},{3,26},{4,29},{5,28},{6,31},{7,30},{8,1},{9,0... | collective-permute-start | bytes 1572872 | tf_op jit(solution)/shard_map/ppermute | solution.py:264
  47.7 0.7 collective-permute-start.8
  48.4 3.6 %collective-permute-done.6 = bf16[256,512]{1,0:T(8,128)(2,1)S(1)} collective-permute-done((bf16[256,512]{1,0:T(8,128)(2,1)}, bf16[256,512]{1,0:T(8,128)(2,1)S(1)}, u32[]{:S(2)}, u32[]{:S(2)}) %collective-permute-start.6) | collective-permute-done | bytes 262176 | tf_op jit(solution)/shard_map/ppermute | solution.py:305
  52.0 1.0 %fusion = bf16[256,512]{1,0:T(8,128)(2,1)S(1)} fusion(bf16[256,512]{1,0:T(8,128)(2,1)S(1)} %collective-permute-done.6, bf16[256,512]{1,0:T(8,128)(2,1)} %get-tuple-element.21), kind=kLoop, calls=%fused_computation.4 | loop fusion | flops 524288 | bytes 786432 | tf_op jit(solution)/shard_map/convert_element_type | solution.py:313
  53.0 0.7 collective-permute-start.7
  53.7 1.3 %collective-permute-start.11 = (bf16[256,512]{1,0:T(8,128)(2,1)S(1)}, bf16[256,512]{1,0:T(8,128)(2,1)S(1)}, u32[]{:S(2)}, u32[]{:S(2)}) collective-permute-start(bf16[256,512]{1,0:T(8,128)(2,1)S(1)} %fusion), channel_id=1, source_target_pairs={{4,0},{5,1},{12,8},{13,9},{20,16},{21,17},{28,24},{29,25}} | collective-permute-start | bytes 786440 | tf_op jit(solution)/shard_map/ppermute | solution.py:305
  55.0 12.3 %collective-permute-done.11 = bf16[256,512]{1,0:T(8,128)(2,1)S(1)} collective-permute-done((bf16[256,512]{1,0:T(8,128)(2,1)S(1)}, bf16[256,512]{1,0:T(8,128)(2,1)S(1)}, u32[]{:S(2)}, u32[]{:S(2)}) %collective-permute-start.11) | collective-permute-done | bytes 262176 | tf_op jit(solution)/shard_map/ppermute | solution.py:305
  67.3 0.2 fusion.5
  67.5 1.5 %collective-permute-start.12 = (bf16[128,512]{1,0:T(8,128)(2,1)S(1)}, bf16[128,512]{1,0:T(8,128)(2,1)S(1)}, u32[]{:S(2)}, u32[]{:S(2)}) collective-permute-start(bf16[128,512]{1,0:T(8,128)(2,1)S(1)} %get-tuple-element.33), channel_id=1, source_target_pairs={{0,24},{1,25},{2,26},{3,27},{4,28},{5,29},{6,30},{7,31},{8,0},{9,1... | collective-permute-start | bytes 393224 | tf_op jit(solution)/shard_map/ppermute | solution.py:264
  69.0 0.8 %collective-permute-start.13 = (bf16[128,512]{1,0:T(8,128)(2,1)S(1)}, bf16[128,512]{1,0:T(8,128)(2,1)S(1)}, u32[]{:S(2)}, u32[]{:S(2)}) collective-permute-start(bf16[128,512]{1,0:T(8,128)(2,1)S(1)} %get-tuple-element.34), channel_id=1, source_target_pairs={{0,25},{1,24},{2,27},{3,26},{4,29},{5,28},{6,31},{7,30},{8,1},{9,0... | collective-permute-start | bytes 393224 | tf_op jit(solution)/shard_map/ppermute | solution.py:264
  69.8 1.2 %maximum_select_fusion = bf16[1,128,4096]{2,1,0:T(8,128)(2,1)} fusion(bf16[1,128,2048]{2,1,0:T(8,128)(2,1)S(1)} %bitcast.49, bf16[1,128,2048]{2,1,0:T(8,128)(2,1)S(1)} %bitcast.48, pred[]{:T(512)S(6)} %eq.13), kind=kLoop, calls=%fused_computation.1 | loop fusion | flops 4718592 | bytes 2097153 | tf_op jit(solution)/shard_map/jit(_where)/select_n | solution.py:328
  71.0 2.1 %collective-permute-done.12 = bf16[128,512]{1,0:T(8,128)(2,1)S(1)} collective-permute-done((bf16[128,512]{1,0:T(8,128)(2,1)S(1)}, bf16[128,512]{1,0:T(8,128)(2,1)S(1)}, u32[]{:S(2)}, u32[]{:S(2)}) %collective-permute-start.12) | collective-permute-done | bytes 131104 | tf_op jit(solution)/shard_map/ppermute | solution.py:264
  73.1 1.2 %collective-permute-done.13 = bf16[128,512]{1,0:T(8,128)(2,1)S(1)} collective-permute-done((bf16[128,512]{1,0:T(8,128)(2,1)S(1)}, bf16[128,512]{1,0:T(8,128)(2,1)S(1)}, u32[]{:S(2)}, u32[]{:S(2)}) %collective-permute-start.13) | collective-permute-done | bytes 131104 | tf_op jit(solution)/shard_map/ppermute | solution.py:264
  74.3 0.7 maximum_select_fusion.2
  75.0 0.7 maximum_select_fusion.1
  (30 shorter events, 0.5 us)
Async XLA Ops:
  1.6 5.4 %collective-permute-start.1 = (bf16[128,512]{1,0:T(8,128)(2,1)S(1)}, bf16[128,512]{1,0:T(8,128)(2,1)S(1)}, u32[]{:S(2)}, u32[]{:S(2)}) collective-permute-start(bf16[128,512]{1,0:T(8,128)(2,1)S(1)} %pad_maximum_fusion.2), channel_id=1, source_target_pairs={{0,1},{1,0},{2,3},{3,2},{4,5},{5,4},{6,7},{7,6},{8,9},{9,8},{10,11... | collective-permute-start | bytes 393224 | tf_op jit(solution)/shard_map/ppermute | solution.py:278
  5.0 12.5 %copy-start.2 = (s32[1,1,4]{2,1,0:T(1,128)S(1)}, s32[1,1,4]{2,1,0:T(1,128)}, u32[]{:S(2)}) copy-start(s32[1,1,4]{2,1,0:T(1,128)} %param.12) | copy-start | bytes 52
  5.1 12.5 %copy-start.3 = (s32[1,128]{1,0:T(1,128)S(1)}, s32[1,128]{1,0:T(1,128)}, u32[]{:S(2)}) copy-start(s32[1,128]{1,0:T(1,128)} %refs_3_.1) | copy-start | bytes 1540
  7.0 23.5 %collective-permute-start.2 = (bf16[128,4096]{1,0:T(8,128)(2,1)S(1)}, bf16[128,4096]{1,0:T(8,128)(2,1)S(1)}, u32[]{:S(2)}, u32[]{:S(2)}) collective-permute-start(bf16[128,4096]{1,0:T(8,128)(2,1)S(1)} %pad_maximum_fusion), channel_id=1, source_target_pairs={{0,1},{1,0},{2,3},{3,2},{4,5},{5,4},{6,7},{7,6},{8,9},{9,8},{10,11... | collective-permute-start | bytes 3145736 | tf_op jit(solution)/shard_map/ppermute | solution.py:283
  8.1 22.3 %copy-start.1 = (bf16[256,512]{1,0:T(8,128)(2,1)}, bf16[256,512]{1,0:T(8,128)(2,1)S(1)}, u32[]{:S(2)}) copy-start(bf16[256,512]{1,0:T(8,128)(2,1)S(1)} %pad_maximum_fusion.1.refs_11_) | copy-start | bytes 786436
  8.1 22.3 %collective-permute-start.5 = (bf16[256,512]{1,0:T(8,128)(2,1)S(1)}, bf16[256,512]{1,0:T(8,128)(2,1)S(1)}, u32[]{:S(2)}, u32[]{:S(2)}) collective-permute-start(bf16[256,512]{1,0:T(8,128)(2,1)S(1)} %pad_maximum_fusion.1.refs_11_), channel_id=1, source_target_pairs={{0,2},{1,3},{2,4},{3,5},{4,6},{5,7},{8,10},{9,11},{10,12},{11,13},... | collective-permute-start | bytes 786440 | tf_op jit(solution)/shard_map/ppermute | solution.py:287
  11.4 19.0 %collective-permute-start.4 = (bf16[256,512]{1,0:T(8,128)(2,1)S(1)}, bf16[256,512]{1,0:T(8,128)(2,1)S(1)}, u32[]{:S(2)}, u32[]{:S(2)}) collective-permute-start(bf16[256,512]{1,0:T(8,128)(2,1)S(1)} %pad_maximum_fusion.1.refs_11_), channel_id=1, source_target_pairs={{0,4},{1,5},{2,6},{3,7},{8,12},{9,13},{10,14},{11,15},{16,20},{17,... | collective-permute-start | bytes 786440 | tf_op jit(solution)/shard_map/ppermute | solution.py:287
  15.6 14.8 %collective-permute-start.3 = (bf16[256,512]{1,0:T(8,128)(2,1)S(1)}, bf16[256,512]{1,0:T(8,128)(2,1)S(1)}, u32[]{:S(2)}, u32[]{:S(2)}) collective-permute-start(bf16[256,512]{1,0:T(8,128)(2,1)S(1)} %pad_maximum_fusion.1.refs_11_), channel_id=1, source_target_pairs={{0,6},{1,7},{8,14},{9,15},{16,22},{17,23},{24,30},{25,31}} | collective-permute-start | bytes 786440 | tf_op jit(solution)/shard_map/ppermute | solution.py:287
  17.6 12.8 %collective-permute-start = (s32[1,133]{1,0:T(1,128)S(1)}, s32[1,133]{1,0:T(1,128)S(1)}, u32[]{:S(2)}, u32[]{:S(2)}) collective-permute-start(s32[1,133]{1,0:T(1,128)S(1)} %bitcast.52), channel_id=1, source_target_pairs={{0,1},{1,0},{2,3},{3,2},{4,5},{5,4},{6,7},{7,6},{8,9},{9,8},{10,11... | collective-permute-start | bytes 1604 | tf_op jit(solution)/shard_map/ppermute | solution.py:277
  30.4 0.6 copy-start.8
  30.4 0.7 copy-start.5
  30.4 0.8 %copy-start.6 = (bf16[256,512]{1,0:T(8,128)(2,1)}, bf16[256,512]{1,0:T(8,128)(2,1)S(1)}, u32[]{:S(2)}) copy-start(bf16[256,512]{1,0:T(8,128)(2,1)S(1)} %collective-permute-done.4.refs_9_) | copy-start | bytes 786436
  30.4 0.9 %copy-start.7 = (bf16[256,512]{1,0:T(8,128)(2,1)}, bf16[256,512]{1,0:T(8,128)(2,1)S(1)}, u32[]{:S(2)}) copy-start(bf16[256,512]{1,0:T(8,128)(2,1)S(1)} %collective-permute-done.3.refs_8_) | copy-start | bytes 786436
  30.5 1.2 %copy-start.4 = (bf16[128,4096]{1,0:T(8,128)(2,1)}, bf16[128,4096]{1,0:T(8,128)(2,1)S(1)}, u32[]{:S(2)}) copy-start(bf16[128,4096]{1,0:T(8,128)(2,1)S(1)} %collective-permute-done.2.refs_7_) | copy-start | bytes 3145732
  42.9 24.4 %copy-start = (f32[256,512]{1,0:T(8,128)S(1)}, f32[256,512]{1,0:T(8,128)}, u32[]{:S(2)}) copy-start(f32[256,512]{1,0:T(8,128)} %get-tuple-element.29) | copy-start | bytes 1572868
  42.9 9.1 %collective-permute-start.6 = (bf16[256,512]{1,0:T(8,128)(2,1)}, bf16[256,512]{1,0:T(8,128)(2,1)S(1)}, u32[]{:S(2)}, u32[]{:S(2)}) collective-permute-start(bf16[256,512]{1,0:T(8,128)(2,1)} %get-tuple-element.22), channel_id=1, source_target_pairs={{2,0},{3,1},{4,2},{5,3},{6,4},{7,5},{10,8},{11,9},{12,10},{13,11},... | collective-permute-start | bytes 786440 | tf_op jit(solution)/shard_map/ppermute | solution.py:305
  44.4 22.9 %collective-permute-start.9 = (bf16[128,2048]{1,0:T(8,128)(2,1)}, bf16[128,2048]{1,0:T(8,128)(2,1)S(1)}, u32[]{:S(2)}, u32[]{:S(2)}) collective-permute-start(bf16[128,2048]{1,0:T(8,128)(2,1)} %get-tuple-element.24), channel_id=1, source_target_pairs={{0,24},{1,25},{2,26},{3,27},{4,28},{5,29},{6,30},{7,31},{8,0},{9,1... | collective-permute-start | bytes 1572872 | tf_op jit(solution)/shard_map/ppermute | solution.py:264
  46.6 20.7 %collective-permute-start.10 = (bf16[128,2048]{1,0:T(8,128)(2,1)}, bf16[128,2048]{1,0:T(8,128)(2,1)S(1)}, u32[]{:S(2)}, u32[]{:S(2)}) collective-permute-start(bf16[128,2048]{1,0:T(8,128)(2,1)} %get-tuple-element.25), channel_id=1, source_target_pairs={{0,25},{1,24},{2,27},{3,26},{4,29},{5,28},{6,31},{7,30},{8,1},{9,0... | collective-permute-start | bytes 1572872 | tf_op jit(solution)/shard_map/ppermute | solution.py:264
  47.7 7.3 %collective-permute-start.8 = (bf16[256,512]{1,0:T(8,128)(2,1)}, bf16[256,512]{1,0:T(8,128)(2,1)S(1)}, u32[]{:S(2)}, u32[]{:S(2)}) collective-permute-start(bf16[256,512]{1,0:T(8,128)(2,1)} %get-tuple-element.21), channel_id=1, source_target_pairs={{6,2},{7,3},{14,10},{15,11},{22,18},{23,19},{30,26},{31,27}} | collective-permute-start | bytes 786440 | tf_op jit(solution)/shard_map/ppermute | solution.py:305
  53.0 2.0 %collective-permute-start.7 = (bf16[256,512]{1,0:T(8,128)(2,1)}, bf16[256,512]{1,0:T(8,128)(2,1)S(1)}, u32[]{:S(2)}, u32[]{:S(2)}) collective-permute-start(bf16[256,512]{1,0:T(8,128)(2,1)} %get-tuple-element.23), channel_id=1, source_target_pairs={{6,4},{7,5},{14,12},{15,13},{22,20},{23,21},{30,28},{31,29}} | collective-permute-start | bytes 786440 | tf_op jit(solution)/shard_map/ppermute | solution.py:305
  53.7 13.6 %collective-permute-start.11 = (bf16[256,512]{1,0:T(8,128)(2,1)S(1)}, bf16[256,512]{1,0:T(8,128)(2,1)S(1)}, u32[]{:S(2)}, u32[]{:S(2)}) collective-permute-start(bf16[256,512]{1,0:T(8,128)(2,1)S(1)} %fusion), channel_id=1, source_target_pairs={{4,0},{5,1},{12,8},{13,9},{20,16},{21,17},{28,24},{29,25}} | collective-permute-start | bytes 786440 | tf_op jit(solution)/shard_map/ppermute | solution.py:305
  67.5 5.5 %collective-permute-start.12 = (bf16[128,512]{1,0:T(8,128)(2,1)S(1)}, bf16[128,512]{1,0:T(8,128)(2,1)S(1)}, u32[]{:S(2)}, u32[]{:S(2)}) collective-permute-start(bf16[128,512]{1,0:T(8,128)(2,1)S(1)} %get-tuple-element.33), channel_id=1, source_target_pairs={{0,24},{1,25},{2,26},{3,27},{4,28},{5,29},{6,30},{7,31},{8,0},{9,1... | collective-permute-start | bytes 393224 | tf_op jit(solution)/shard_map/ppermute | solution.py:264
  69.0 5.3 %collective-permute-start.13 = (bf16[128,512]{1,0:T(8,128)(2,1)S(1)}, bf16[128,512]{1,0:T(8,128)(2,1)S(1)}, u32[]{:S(2)}, u32[]{:S(2)}) collective-permute-start(bf16[128,512]{1,0:T(8,128)(2,1)S(1)} %get-tuple-element.34), channel_id=1, source_target_pairs={{0,25},{1,24},{2,27},{3,26},{4,29},{5,28},{6,31},{7,30},{8,1},{9,0... | collective-permute-start | bytes 393224 | tf_op jit(solution)/shard_map/ppermute | solution.py:264
